TPU v7x, 32 devices: a whole 2x2x4 slice. The times are simulated.
32 devices in a mesh: grp: 1, col: 32 (over z, y, x, core).
Axes of the slice: x: 2, y: 2, z: 4, core: 2. Of those that a mesh axis runs over, the one named last changes fastest.
Arguments:
- pair: bfloat16 [16, 1024, 128], P('grp', 'col'), may hold values from -6 to 6
- w_query: bfloat16 [128, 128], replicated, may hold values from -0.5 to 0.5
- w_kv: bfloat16 [128, 256], replicated, may hold values from -0.5 to 0.5
- w_gate: bfloat16 [128, 128], replicated, may hold values from -0.5 to 0.5
- w_out: bfloat16 [128, 128], replicated, may hold values from -0.5 to 0.5
- pair_bias: bfloat16 [4, 1024, 1024], P('grp', 'col'), may hold values from -8 to 300
- lengths: int32 [1], P('grp'), may hold values from 512 to 1024
Outputs:
- update: bfloat16 [16, 1024, 128], P('grp', 'col')
All inputs are finite; a program needn't handle non-finite values.
Results may differ from a plain program's by a relative error of at most 0.0081.
Values may be sent and summed in bfloat16 or wider, within the bound.
A program may use at most 128 MiB of HBM per device.

v0:
```python
import jax
import jax.numpy as jnp
from jax import lax
from jax.sharding import PartitionSpec as P

HEADS = 4


def normalize(pair_block):
    values_f = pair_block.astype(jnp.float32)
    mean_val = jnp.mean(values_f, axis=-1, keepdims=True)
    centred = values_f - mean_val
    variance = jnp.mean(centred * centred, axis=-1, keepdims=True)
    return (centred * lax.rsqrt(variance + 1e-05)).astype(jnp.bfloat16)


def attend(normed, bias_query, key_limit, w_query, w_kv, w_gate, w_out, gather_keys):
    row_count, col_count, chan_count = normed.shape
    head_width = chan_count // HEADS
    queries = (
        jnp.dot(normed, w_query, preferred_element_type=jnp.float32) * head_width ** (-0.5)
    ).astype(jnp.bfloat16)
    queries = queries.reshape(row_count, col_count, HEADS, head_width)
    gate_act = jax.nn.sigmoid(jnp.dot(normed, w_gate, preferred_element_type=jnp.float32))

    def consume(running, segment, offset):
        run_max, run_sum, run_acc = running
        key_value = jnp.dot(segment, w_kv, preferred_element_type=jnp.float32).astype(jnp.bfloat16)
        tile_len = key_value.shape[1]
        key_tile = key_value[:, :, :chan_count].reshape(row_count, tile_len, HEADS, head_width)
        value_tile = key_value[:, :, chan_count:].reshape(row_count, tile_len, HEADS, head_width)
        scores = jnp.einsum(
            "rjhd,rkhd->rhjk", queries, key_tile, preferred_element_type=jnp.float32
        )
        bias_part = lax.dynamic_slice_in_dim(bias_query, offset, tile_len, 2).astype(jnp.float32)
        key_pos = offset + jnp.arange(tile_len, dtype=jnp.int32)
        key_mask = jnp.where(key_pos < key_limit, 0.0, -1000000000.0).astype(jnp.float32)
        scores = scores + bias_part[None] + key_mask
        new_max = jnp.maximum(run_max, jnp.max(scores, axis=-1))
        rescale = jnp.exp(run_max - new_max)
        expon = jnp.exp(scores - new_max[..., None])
        new_sum = run_sum * rescale + jnp.sum(expon, axis=-1)
        weights = expon.astype(jnp.bfloat16)
        partial_out = jnp.einsum(
            "rhjk,rkhd->rjhd", weights, value_tile, preferred_element_type=jnp.float32
        )
        new_acc = run_acc * jnp.transpose(rescale, (0, 2, 1))[..., None] + partial_out
        return (new_max, new_sum, new_acc)

    def fold_piece(running, segment, offset, project):
        tile_len = segment.shape[1]
        block_len = 512
        block_num = tile_len // block_len
        blocks = jnp.moveaxis(
            segment.reshape(row_count, block_num, block_len, segment.shape[2]), 1, 0
        )

        def advance(state_now, item_pair):
            block_tile, block_idx = item_pair
            return (consume(state_now, block_tile, block_idx * block_len), None)

        final_state, unused = lax.scan(
            advance, running, (blocks, jnp.arange(block_num, dtype=jnp.int32))
        )
        return final_state

    initial = (
        jnp.full((row_count, HEADS, col_count), -1e30, jnp.float32),
        jnp.zeros((row_count, HEADS, col_count), jnp.float32),
        jnp.zeros((row_count, col_count, HEADS, head_width), jnp.float32),
    )
    run_max, run_sum, run_acc = gather_keys(fold_piece, initial)
    attended = run_acc / jnp.transpose(run_sum, (0, 2, 1))[..., None]
    hidden = (gate_act * attended.reshape(row_count, col_count, chan_count)).astype(jnp.bfloat16)
    return jnp.dot(hidden, w_out, preferred_element_type=jnp.float32).astype(jnp.bfloat16)


def on_device(pair, w_query, w_kv, w_gate, w_out, pair_bias, lengths):
    key_limit = lengths[0]
    normed = normalize(pair)
    received = lax.all_to_all(pair_bias, "col", split_axis=2, concat_axis=1, tiled=True)
    bias_query = jnp.transpose(received, (0, 2, 1))

    def gather_keys(fold_piece, initial):
        return fold_piece(
            initial, lax.all_gather(normed, "col", axis=1, tiled=True), jnp.int32(0), True
        )

    return attend(normed, bias_query, key_limit, w_query, w_kv, w_gate, w_out, gather_keys)


def solution(mesh):
    in_specs = (P("grp", "col", None), P(), P(), P(), P(), P("grp", "col", None), P("grp"))
    out_specs = P("grp", "col", None)
    return jax.shard_map(
        on_device, mesh=mesh, in_specs=in_specs, out_specs=out_specs, check_vma=False
    )
```

profile of v0, /device:TPU:0, one launch (start us, length us, event | category | flops | bytes accessed | tf_op | source)
XLA Modules:
  0.0 114.7 jit_solution(4545162258831155141)
XLA Ops:
  6.5 1.1 convert_reduce_fusion
  7.6 1.2 %fusion.30 = f32[16,32]{1,0:T(8,128)S(1)} fusion(bf16[16,32,128]{2,1,0:T(8,128)(2,1)} %param.9, f32[16,32]{1,0:T(8,128)S(1)} %broadcast_multiply_fusion), kind=kLoop, calls=%fused_computation.40 | loop fusion | flops 261632 | bytes 135168 | tf_op jit(solution)/shard_map/reduce_sum | solution.py:13
  8.8 1.8 %fusion.31 = bf16[16,32,128]{2,1,0:T(8,128)(2,1)} fusion(bf16[16,32,128]{2,1,0:T(8,128)(2,1)} %param.9, f32[16,32]{1,0:T(8,128)S(1)} %add_rsqrt_fusion, f32[16,32]{1,0:T(8,128)S(1)} %broadcast_multiply_fusion), kind=kLoop, calls=%fused_computation.41 | loop fusion | flops 262144 | bytes 266240 | tf_op jit(solution)/shard_map/convert_element_type | solution.py:14
  10.6 1.6 %copy.17 = bf16[4,32,1024]{1,0,2:T(4,128)(2,1)S(1)} copy(bf16[4,32,1024]{2,1,0:T(8,128)(2,1)} %param.14) | data formatting | bytes 524288 | tf_op args[5]
  12.2 1.7 %reshape.48 = bf16[32,2,2048]{2,1,0:T(2,128)(2,1)} reshape(bf16[1024,4,32]{2,1,0:T(4,128)(2,1)S(1)} %bitcast.92) | data formatting | bytes 524288
  13.9 7.3 %all-to-all-start = ((bf16[32,2,2048]{2,1,0:T(2,128)(2,1)}), bf16[32,2,2048]{2,1,0:T(2,128)(2,1)S(1)}, u32[]{:S(2)}, u32[]{:S(2)}) async-start(bf16[32,2,2048]{2,1,0:T(2,128)(2,1)} %reshape.48), calls=%async_computation | async-start | bytes 524288 | tf_op jit(solution)/shard_map/all_to_all | solution.py:81
  21.2 1.1 fusion.27
  22.6 0.9 copy.21
  23.5 0.7 copy.20
  24.2 8.9 %all-to-all-done = bf16[32,2,2048]{2,1,0:T(2,128)(2,1)S(1)} async-done(((bf16[32,2,2048]{2,1,0:T(2,128)(2,1)}), bf16[32,2,2048]{2,1,0:T(2,128)(2,1)S(1)}, u32[]{:S(2)}, u32[]{:S(2)}) %all-to-all-start) | async-done | bytes 262176 | tf_op jit(solution)/shard_map/all_to_all | solution.py:81
  34.3 1.1 all_to_all.16
  35.4 43.4 %all-gather.2.cloned.1.call-done = bf16[16,1024,128]{2,1,0:T(8,128)(2,1)} async-done(((bf16[16,32,128]{2,1,0:T(8,128)(2,1)}), bf16[16,1024,128]{2,1,0:T(8,128)(2,1)}) %all-gather.2.cloned.1.call-update) | async-done | bytes 4194320 | tf_op jit(solution)/shard_map/all_gather | solution.py:86
  78.8 26.5 %while.15 = (s32[]{:T(128)}, f32[16,4,32]{2,1,0:T(4,128)S(1)}, f32[16,4,32]{2,1,0:T(4,128)S(1)}, f32[16,32,4,32]{1,3,2,0:T(8,128)S(1)}, bf16[2,16,512,128]{3,2,0...) while((s32[]{:T(128)}, f32[16,4,32]{2,1,0:T(4,128)S(1)}, ...), condition=%wide.region_5.6_spmd.clone, body=%wide.region_2.5_spmd.clone.sunk | while | flops 684996096 | bytes 52896580 | solution.py:62
  80.7 2.9 %convolution_convert_fusion.3 = bf16[16,512,256]{1,2,0:T(8,128)(2,1)S(1)} fusion(bf16[2,16,512,128]{3,2,0,1:T(8,128)(2,1)} %get-tuple-element.254, s32[]{:T(128)} %get-tuple-element.236, bf16[128,256]{0,1:T(8,128)(2,1)} %get-tuple-element.255), kind=kOutput, calls=%fused_computation.6.clone.1 | convolution fusion | flops 538968064 | bytes 6357504 | tf_op jit(solution)/shard_map/while/body/eval_jaxpr/dot_general | solution.py:28
  83.9 0.7 copy-done.2
  84.6 2.7 %fusion.65 = (f32[16,4,32]{2,1,0:T(4,128)S(1)}, f32[16,4,512,32]{2,3,1,0:T(8,128)}) fusion(f32[512]{0:T(512)S(1)} %fusion.63, f32[4,32,512]{2,1,0:T(8,128)S(1)} %dynamic-slice_convert_fusion.2, bf16[16,32,4,32]{3,1,2,0:T(8,128)(2,1)S(1)} %copy-done.2, bf16[16,512,4,32]{1,3,2,0:T(8,128)(2,1)S(1)} %bitcast.90), kind=kOutput, calls=%fused_computation.5.clone.1 | convolution fusion | flops 70252544 | bytes 6694912 | tf_op jit(solution)/shard_map/while/body/eval_jaxpr/rjhd,rkhd->rhjk/dot_general | solution.py:32
  87.4 3.4 %fusion.69 = f32[16,32,4,32]{1,3,2,0:T(8,128)S(1)} fusion(bf16[16,512,4,32]{1,3,2,0:T(8,128)(2,1)S(1)} %bitcast.89, f32[16,4,512,32]{2,3,1,0:T(8,128)} %get-tuple-element.219, f32[16,4,32]{2,1,0:T(4,128)S(1)} %get-tuple-element.251, f32[512]{0:T(512)S(1)} %fusion.63, f32[4,32,512]{2,1,0:T(8,128)S(1)} %dynamic-slice_convert_fusion.2, ...), kind=kOutput, calls=%fused_computation.14.clone.1 | convolution fusion | flops 71499776 | bytes 7096321 | tf_op jit(solution)/shard_map/while/body/eval_jaxpr/rhjk,rkhd->rjhd/dot_general | solution.py:44
  90.8 1.2 %fusion.67 = f32[16,4,32]{2,1,0:T(4,128)S(1)} fusion(f32[16,4,512,32]{2,3,1,0:T(8,128)S(1)} %copy-done.1, f32[16,4,32]{2,1,0:T(4,128)S(1)} %get-tuple-element.251, f32[512]{0:T(512)S(1)} %fusion.63, f32[4,32,512]{2,1,0:T(8,128)S(1)} %dynamic-slice_convert_fusion.2), kind=kLoop, calls=%fused_computation.4.clone.1 | loop fusion | flops 4192256 | bytes 4474880 | tf_op jit(solution)/shard_map/while/body/eval_jaxpr/reduce_sum | solution.py:42
  94.0 2.9 %convolution_convert_fusion.3 = bf16[16,512,256]{1,2,0:T(8,128)(2,1)S(1)} fusion(bf16[2,16,512,128]{3,2,0,1:T(8,128)(2,1)} %get-tuple-element.254, s32[]{:T(128)} %get-tuple-element.236, bf16[128,256]{0,1:T(8,128)(2,1)} %get-tuple-element.255), kind=kOutput, calls=%fused_computation.6.clone.1 | convolution fusion | flops 538968064 | bytes 6357504 | tf_op jit(solution)/shard_map/while/body/eval_jaxpr/dot_general | solution.py:28
  97.2 0.7 copy-done.2
  97.9 2.7 %fusion.65 = (f32[16,4,32]{2,1,0:T(4,128)S(1)}, f32[16,4,512,32]{2,3,1,0:T(8,128)}) fusion(f32[512]{0:T(512)S(1)} %fusion.63, f32[4,32,512]{2,1,0:T(8,128)S(1)} %dynamic-slice_convert_fusion.2, bf16[16,32,4,32]{3,1,2,0:T(8,128)(2,1)S(1)} %copy-done.2, bf16[16,512,4,32]{1,3,2,0:T(8,128)(2,1)S(1)} %bitcast.90), kind=kOutput, calls=%fused_computation.5.clone.1 | convolution fusion | flops 70252544 | bytes 6694912 | tf_op jit(solution)/shard_map/while/body/eval_jaxpr/rjhd,rkhd->rhjk/dot_general | solution.py:32
  100.7 3.4 %fusion.69 = f32[16,32,4,32]{1,3,2,0:T(8,128)S(1)} fusion(bf16[16,512,4,32]{1,3,2,0:T(8,128)(2,1)S(1)} %bitcast.89, f32[16,4,512,32]{2,3,1,0:T(8,128)} %get-tuple-element.219, f32[16,4,32]{2,1,0:T(4,128)S(1)} %get-tuple-element.251, f32[512]{0:T(512)S(1)} %fusion.63, f32[4,32,512]{2,1,0:T(8,128)S(1)} %dynamic-slice_convert_fusion.2, ...), kind=kOutput, calls=%fused_computation.14.clone.1 | convolution fusion | flops 71499776 | bytes 7096321 | tf_op jit(solution)/shard_map/while/body/eval_jaxpr/rhjk,rkhd->rjhd/dot_general | solution.py:44
  104.1 1.2 %fusion.67 = f32[16,4,32]{2,1,0:T(4,128)S(1)} fusion(f32[16,4,512,32]{2,3,1,0:T(8,128)S(1)} %copy-done.1, f32[16,4,32]{2,1,0:T(4,128)S(1)} %get-tuple-element.251, f32[512]{0:T(512)S(1)} %fusion.63, f32[4,32,512]{2,1,0:T(8,128)S(1)} %dynamic-slice_convert_fusion.2), kind=kLoop, calls=%fused_computation.4.clone.1 | loop fusion | flops 4192256 | bytes 4474880 | tf_op jit(solution)/shard_map/while/body/eval_jaxpr/reduce_sum | solution.py:42
  105.9 1.9 %convolution_convert_fusion.1 = bf16[16,32,128]{2,1,0:T(8,128)(2,1)} fusion(f32[16,32,128]{2,1,0:T(8,128)S(1)} %copy.23, bf16[16,32,128]{2,1,0:T(8,128)(2,1)} %fusion.31, bf16[128,128]{1,0:T(8,128)(2,1)} %param.13, bf16[128,128]{1,0:T(8,128)(2,1)} %param.12), kind=kOutput, calls=%fused_computation.34 | convolution fusion | flops 33947648 | bytes 589824 | tf_op jit(solution)/shard_map/dot_general | solution.py:75
  (45 shorter events, 5.3 us)
Async XLA Ops:
  6.5 14.7 %copy-start = (bf16[128,128]{1,0:T(8,128)(2,1)S(1)}, bf16[128,128]{1,0:T(8,128)(2,1)}, u32[]{:S(2)}) copy-start(bf16[128,128]{1,0:T(8,128)(2,1)} %param.10) | copy-start | bytes 98308
  6.5 17.0 %copy-start.5 = (bf16[128,256]{1,0:T(8,128)(2,1)S(1)}, bf16[128,256]{1,0:T(8,128)(2,1)}, u32[]{:S(2)}) copy-start(bf16[128,256]{1,0:T(8,128)(2,1)} %param.11) | copy-start | bytes 196612
  6.5 72.3 %all-gather.2.cloned.1.call-start = ((), (), s32[]{:S(2)}) async-start(), calls=%async_computation.1 | async-start | bytes 4325376 | tf_op jit(solution)/shard_map/all_gather | solution.py:86
  13.9 19.2 %all-to-all-start = ((bf16[32,2,2048]{2,1,0:T(2,128)(2,1)}), bf16[32,2,2048]{2,1,0:T(2,128)(2,1)S(1)}, u32[]{:S(2)}, u32[]{:S(2)}) async-start(bf16[32,2,2048]{2,1,0:T(2,128)(2,1)} %reshape.48), calls=%async_computation | async-start | bytes 524288 | tf_op jit(solution)/shard_map/all_to_all | solution.py:81
  78.8 1.9 %copy-start.3 = (bf16[4,32,1024]{2,1,0:T(8,128)(2,1)}, bf16[4,32,1024]{2,1,0:T(8,128)(2,1)S(1)}, u32[]{:S(2)}) copy-start(bf16[4,32,1024]{2,1,0:T(8,128)(2,1)S(1)} %get-tuple-element.258) | copy-start | bytes 786436 | tf_op jit(solution)/shard_map/while
  83.6 1.0 copy-start.2
  87.4 3.5 %copy-start.1 = (f32[16,4,512,32]{2,3,1,0:T(8,128)S(1)}, f32[16,4,512,32]{2,3,1,0:T(8,128)}, u32[]{:S(2)}) copy-start(f32[16,4,512,32]{2,3,1,0:T(8,128)} %get-tuple-element.219) | copy-start | bytes 12582916 | tf_op jit(solution)/shard_map/while
  90.8 1.3 %copy-start.4 = (bf16[4,32,1024]{2,1,0:T(8,128)(2,1)S(1)}, bf16[4,32,1024]{2,1,0:T(8,128)(2,1)}, u32[]{:S(2)}) copy-start(bf16[4,32,1024]{2,1,0:T(8,128)(2,1)} %copy-done.3) | copy-start | bytes 786436 | tf_op jit(solution)/shard_map/while
  92.1 1.9 %copy-start.3 = (bf16[4,32,1024]{2,1,0:T(8,128)(2,1)}, bf16[4,32,1024]{2,1,0:T(8,128)(2,1)S(1)}, u32[]{:S(2)}) copy-start(bf16[4,32,1024]{2,1,0:T(8,128)(2,1)S(1)} %get-tuple-element.258) | copy-start | bytes 786436 | tf_op jit(solution)/shard_map/while
  96.9 1.0 copy-start.2
  100.7 3.5 %copy-start.1 = (f32[16,4,512,32]{2,3,1,0:T(8,128)S(1)}, f32[16,4,512,32]{2,3,1,0:T(8,128)}, u32[]{:S(2)}) copy-start(f32[16,4,512,32]{2,3,1,0:T(8,128)} %get-tuple-element.219) | copy-start | bytes 12582916 | tf_op jit(solution)/shard_map/while
  104.1 1.3 %copy-start.4 = (bf16[4,32,1024]{2,1,0:T(8,128)(2,1)S(1)}, bf16[4,32,1024]{2,1,0:T(8,128)(2,1)}, u32[]{:S(2)}) copy-start(bf16[4,32,1024]{2,1,0:T(8,128)(2,1)} %copy-done.3) | copy-start | bytes 786436 | tf_op jit(solution)/shard_map/while
Sparse Core Ops, SparseCore 0:
  10.7 68.0 all-gather.1
where the time goes:
time: 115 us
  waiting for transfers between devices  52.3 us (45%)
  matrix products  21.1 us (18%)
  between operations  13.5 us (12%)
  local copies, waits for them, and re-layouts  11.1 us (10%)
  other arithmetic  8.07 us (7%)
  starting transfers between devices  7.3 us (6%)
  loops' own time  1.31 us (1%)
    all_gather x1, waiting for transfers between devices, gather_keys(): lax.all_gather(normed, 'col', axis=1, tiled=True)  43.4 us
    all_to_all x1, waiting for transfers between devices, on_device(): lax.all_to_all(pair_bias, 'col', split_axis=2, concat_axis=1, tiled=True)  8.85 us
    all_to_all x1, starting transfers between devices, on_device(): lax.all_to_all(pair_bias, 'col', split_axis=2, concat_axis=1, tiled=True)  7.3 us
    dot_general x2, matrix products, consume(): jnp.einsum('rhjk,rkhd->rjhd', weights, value_tile, preferred_element_type...  6.84 us
    dot_general x2, matrix products, consume(): jnp.dot(segment, w_kv, preferred_element_type=jnp.float32)  5.72 us
    dot_general x2, matrix products, consume(): jnp.einsum('rjhd,rkhd->rhjk', queries, key_tile, preferred_element_type=j...  5.49 us
    unnamed x9, local copies, waits for them, and re-layouts  5.46 us
    reduce_sum x2, other arithmetic, consume(): new_sum = run_sum * rescale + jnp.sum(expon, axis=-1)  2.38 us
  transfers between devices with their start and end apart: 2, of which 2 were waited for; matrix products, arithmetic and copies ran while one was open for 7% of the time, Pallas kernels for 0%

commit v1 on v0

v1 whole, which is shorter than its diff:
```python
import functools

import jax
import jax.numpy as jnp
from jax import lax
from jax.experimental import pallas as pl
from jax.experimental.pallas import tpu as pltpu
from jax.sharding import PartitionSpec as P

HEADS = 4
MESH = pl.DeviceIdType.MESH
F32 = jnp.float32
BF16 = jnp.bfloat16
LOG2E = 1.4426950408889634
NT = (((1,), (1,)), ((), ()))
TN = (((0,), (0,)), ((), ()))


def dot(lhs, rhs):
    return jnp.dot(lhs, rhs, preferred_element_type=F32)


def dot_nt(lhs, rhs):
    return lax.dot_general(lhs, rhs, NT, preferred_element_type=F32)


def transposed(weight):
    return weight.astype(F32).T.astype(BF16)


def body(
    line, pair_ref, wq_ref, wkv_ref, wg_ref, wo_ref, bias_ref, len_ref, out_ref,
    gath, swap, bsend, bgath, bias_f, amat, gate, acc, run_max, run_sum, upd,
    wvt_ref, recv, zsend, nsend, fsend, bs_sem, br_sem, core_s, core_r,
):
    rows, cols, chan = pair_ref.shape
    half_rows, cols2 = rows // 2, 2 * cols
    quarter = half_rows // 2
    width = chan // HEADS
    lanes = HEADS * cols2
    chips = 4 * line

    me = lax.axis_index("col")
    core = lax.rem(me, 2)
    chip = me // 2
    z = chip // 4
    xy = lax.rem(chip, 4)
    sibling = me + 1 - 2 * core
    x_line = xy + 1 - 2 * lax.rem(xy, 2)
    y_line = lax.rem(xy + 2, 4)
    diag = 3 - xy
    near = (x_line, y_line)
    far = (y_line, x_line)

    def device(z_at, xy_at):
        return {"col": (z_at * 4 + xy_at) * 2 + core}

    barrier = pltpu.get_barrier_semaphore()

    def greet(k, carry):
        other = lax.rem(chip + k, chips)
        pl.semaphore_signal(barrier, inc=1, device_id={"col": other * 2 + core}, device_id_type=MESH)
        return carry

    lax.fori_loop(1, chips, greet, 0)
    pl.semaphore_signal(barrier, inc=1, device_id={"col": sibling}, device_id_type=MESH)

    def normalized(first):
        values = pair_ref[pl.ds(first, half_rows)].astype(F32)
        centred = values - jnp.mean(values, axis=-1, keepdims=True)
        variance = jnp.mean(centred * centred, axis=-1, keepdims=True)
        return (centred * lax.rsqrt(variance + 1e-05)).astype(BF16)

    own_cols = pl.ds(pl.multiple_of(core * cols, cols), cols)
    swap[...] = normalized((1 - core) * half_rows)
    gath[xy, z, :, own_cols, :] = normalized(core * half_rows)

    pl.semaphore_wait(barrier, chips)

    swap_copy = pltpu.make_async_remote_copy(
        src_ref=swap, dst_ref=gath.at[xy, z, :, own_cols, :],
        send_sem=core_s.at[0], recv_sem=core_r.at[0],
        device_id={"col": sibling}, device_id_type=MESH,
    )
    swap_copy.start()

    low = lax.broadcasted_iota(jnp.int32, (cols, 2 * cols2), 1) < cols2
    for pair_at in range(chips // 2):
        parts = [
            bias_ref[h, :, pair_at * 2 * cols2 : (pair_at + 1) * 2 * cols2].astype(F32)
            for h in range(HEADS)
        ]
        rolled = [pltpu.roll(part, cols2, 1) for part in parts]
        for h in range(0, HEADS, 2):
            span = slice(h * cols2, (h + 2) * cols2)
            bsend[2 * pair_at, :, span] = jnp.where(low, parts[h], rolled[h + 1]).astype(BF16)
            bsend[2 * pair_at + 1, :, span] = jnp.where(low, rolled[h], parts[h + 1]).astype(BF16)

    swap_copy.wait_recv()

    def block_copy(half, xy_at, z_at, target, send_sem):
        block = gath.at[xy_at, z_at, pl.ds(half * quarter, quarter)]
        return pltpu.make_async_remote_copy(
            src_ref=block, dst_ref=block, send_sem=send_sem, recv_sem=recv.at[half, xy_at, z_at],
            device_id=target, device_id_type=MESH,
        )

    def up(half, z_at):
        return block_copy(half, xy, z_at, device(z + 1, xy), zsend.at[half, 0, z_at])

    def down(half, z_at):
        return block_copy(half, xy, z_at, device(z - 1, xy), zsend.at[half, 1, z_at])

    def to_near(half, z_at):
        return block_copy(half, xy, z_at, device(z, near[half]), nsend.at[half, z_at])

    def to_far(half, which, z_at):
        from_line = (xy, near[half])[which]
        return block_copy(half, from_line, z_at, device(z, far[half]), fsend.at[half, which, z_at])

    def arrived(half, xy_at, z_at):
        block_copy(half, xy_at, z_at, device(z, near[half]), nsend.at[half, z_at]).wait_recv()

    for half in range(2):
        pl.when(z + 1 < line)(lambda half=half: up(half, z).start())
        pl.when(z > 0)(lambda half=half: down(half, z).start())
        to_near(half, z).start()
        to_far(half, 0, z).start()

    def bias_copy(other, slot):
        return pltpu.make_async_remote_copy(
            src_ref=bsend.at[other], dst_ref=bgath.at[lax.rem(slot, 4), slot // 4, own_cols, :],
            send_sem=bs_sem.at[other], recv_sem=br_sem.at[slot],
            device_id={"col": other * 2 + core}, device_id_type=MESH,
        )

    def send_bias(k, carry):
        bias_copy(lax.rem(chip + k, chips), chip).start()
        return carry

    lax.fori_loop(1, chips, send_bias, 0)
    bgath[xy, z, own_cols, :] = bsend[chip]

    wqt = transposed(wq_ref[...])
    wgt = transposed(wg_ref[...])
    wvt_ref[...] = transposed(wkv_ref[:, chan:])
    w_key = wkv_ref[:, :chan]
    same_head = (
        lax.broadcasted_iota(jnp.int32, (chan, lanes), 0) // width
        == lax.broadcasted_iota(jnp.int32, (chan, lanes), 1) // cols2
    )

    def prepare(r, carry):
        own = gath[xy, z, r]
        repeated = jnp.concatenate([own] * HEADS, axis=0)
        queries = (dot_nt(wqt, repeated) * width ** (-0.5)).astype(BF16).astype(F32)
        queries = jnp.where(same_head, queries, 0.0).astype(BF16)
        amat[r] = (dot(w_key, queries) * LOG2E).astype(BF16)
        gate[r] = jax.nn.sigmoid(dot_nt(wgt, own))
        return carry

    lax.fori_loop(0, half_rows, prepare, 0)

    def pass_far(half, z_at):
        arrived(half, near[half], z_at)
        to_far(half, 1, z_at).start()

    def pass_line(s):
        def lower():
            for half in range(2):
                arrived(half, xy, z - s)
                pl.when(z + 1 < line)(lambda: up(half, z - s).start())
                to_near(half, z - s).start()
                to_far(half, 0, z - s).start()

        def upper():
            for half in range(2):
                arrived(half, xy, z + s)
                pl.when(z > 0)(lambda: down(half, z + s).start())
                to_near(half, z + s).start()
                to_far(half, 0, z + s).start()

        pl.when(z >= s)(lower)
        pl.when(z + s < line)(upper)

    def pass_near(s):
        def lower():
            for half in range(2):
                pass_far(half, z - s)

        def upper():
            for half in range(2):
                pass_far(half, z + s)

        pl.when(z >= s)(lower)
        if s:
            pl.when(z + s < line)(upper)

    for s in range(1, line):
        pass_line(s)
        pass_near(s - 1)
    pass_near(line - 1)

    def wait_bias(k, carry):
        other = lax.rem(chip + k, chips)
        bias_copy(other, other).wait_recv()
        return carry

    lax.fori_loop(1, chips, wait_bias, 0)
    bias_swap = pltpu.make_async_remote_copy(
        src_ref=bgath.at[:, :, own_cols, :], dst_ref=bgath.at[:, :, own_cols, :],
        send_sem=core_s.at[1], recv_sem=core_r.at[1],
        device_id={"col": sibling}, device_id_type=MESH,
    )
    bias_swap.start()
    bias_swap.wait_recv()

    limit = len_ref[0]

    def spread_bias(k, carry):
        line_at, z_at = k // line, lax.rem(k, line)
        first = (z_at * 4 + line_at) * cols2
        position = first + lax.broadcasted_iota(jnp.int32, (cols2, lanes), 0)
        mask = jnp.where(position < limit, 0.0, -1000000000.0)
        bias_f[line_at, z_at] = (bgath[line_at, z_at].astype(F32) + mask) * LOG2E
        return carry

    lax.fori_loop(0, chips, spread_bias, 0)

    run_max[...] = jnp.full_like(run_max, -1e30)
    run_sum[...] = jnp.zeros_like(run_sum)
    acc[...] = jnp.zeros_like(acc)
    group = 4 if line % 4 == 0 else 1
    keys = group * cols2

    def fold(half, lines):
        wvt = wvt_ref[...]

        def one(step, carry):
            r = half * quarter + step // (line // group)
            z_at = pl.ds(lax.rem(step, line // group) * group, group)
            tiles = [gath[at, z_at, r].reshape(keys, chan) for at in lines]
            scores = [
                dot(tile, amat[r]) + bias_f[at, z_at].reshape(keys, lanes)
                for tile, at in zip(tiles, lines)
            ]
            old_max = run_max[r]
            new_max = old_max
            for part in scores:
                new_max = jnp.maximum(new_max, jnp.max(part, axis=0, keepdims=True))
            rescale = jnp.exp2(old_max - new_max)
            total = run_sum[r] * rescale
            result = acc[r] * rescale
            for part, tile in zip(scores, tiles):
                expon = jnp.exp2(part - new_max)
                total = total + jnp.sum(expon, axis=0, keepdims=True)
                result = result + dot(dot_nt(wvt, tile).astype(BF16), expon.astype(BF16))
            run_max[r] = new_max
            run_sum[r] = total
            acc[r] = result
            return carry

        steps = quarter * (line // group)
        lax.fori_loop(0, steps, one, 0, unroll=2)

    def wait_line(half, at):
        for z_at in range(line):
            arrived(half, at, z_at)

    for half in range(2):
        fold(half, (xy, near[half]))
    for half in range(2):
        wait_line(half, far[half])
        fold(half, (far[half],))

    other_cols = pl.ds(pl.multiple_of((1 - core) * cols, cols), cols)

    def out_copy(half):
        return pltpu.make_async_remote_copy(
            src_ref=upd.at[pl.ds(half * quarter, quarter), other_cols, :],
            dst_ref=out_ref.at[pl.ds(core * half_rows + half * quarter, quarter)],
            send_sem=core_s.at[2 + half], recv_sem=core_r.at[2 + half],
            device_id={"col": sibling}, device_id_type=MESH,
        )

    for half in range(2):
        wait_line(half, diag)
        fold(half, (diag,))

        def finish(step, carry):
            r = half * quarter + step
            result = acc[r] / run_sum[r]
            parts = []
            for h in range(HEADS):
                block = result[h * width : (h + 1) * width, (h // 2) * 2 * cols2 : (h // 2 + 1) * 2 * cols2]
                if h % 2:
                    block = pltpu.roll(block, cols2, 1)
                parts.append(block[:, :cols2])
            attended = jnp.concatenate(parts, axis=0)
            hidden = (gate[r] * attended).T.astype(BF16)
            upd[r] = dot(hidden, wo_ref[...]).astype(BF16)
            return carry

        lax.fori_loop(0, quarter, finish, 0, unroll=2)
        out_copy(half).start()
        out_ref[pl.ds(core * half_rows + half * quarter, quarter)] = upd[
            pl.ds(half * quarter, quarter), own_cols, :
        ]

    for half in range(2):
        out_copy(half).wait()
        for z_at in range(line):
            pl.when((z + 1 < line) & (z >= z_at))(lambda: up(half, z_at).wait_send())
            pl.when((z > 0) & (z <= z_at))(lambda: down(half, z_at).wait_send())
            to_near(half, z_at).wait_send()
            to_far(half, 0, z_at).wait_send()
            to_far(half, 1, z_at).wait_send()
    swap_copy.wait_send()
    bias_swap.wait_send()

    def drain_bias(k, carry):
        bias_copy(lax.rem(chip + k, chips), chip).wait_send()
        return carry

    lax.fori_loop(1, chips, drain_bias, 0)


def solution(mesh):
    chips = mesh.shape["col"] // 2
    line = chips // 4

    def on_device(pair, w_query, w_kv, w_gate, w_out, pair_bias, lengths):
        rows, cols, chan = pair.shape
        half_rows, cols2 = rows // 2, 2 * cols
        quarter = half_rows // 2
        lanes = HEADS * cols2
        vmem = pl.BlockSpec(memory_space=pltpu.VMEM)
        dma = pltpu.SemaphoreType.DMA
        return pl.pallas_call(
            functools.partial(body, line),
            out_shape=jax.ShapeDtypeStruct(pair.shape, BF16),
            in_specs=[vmem] * 6 + [pl.BlockSpec(memory_space=pltpu.SMEM)],
            out_specs=vmem,
            scratch_shapes=[
                pltpu.VMEM((4, line, half_rows, cols2, chan), BF16),
                pltpu.VMEM((half_rows, cols, chan), BF16),
                pltpu.VMEM((chips, cols, lanes), BF16),
                pltpu.VMEM((4, line, cols2, lanes), BF16),
                pltpu.VMEM((4, line, cols2, lanes), F32),
                pltpu.VMEM((half_rows, chan, lanes), BF16),
                pltpu.VMEM((half_rows, chan, cols2), F32),
                pltpu.VMEM((half_rows, chan, lanes), F32),
                pltpu.VMEM((half_rows, 1, lanes), F32),
                pltpu.VMEM((half_rows, 1, lanes), F32),
                pltpu.VMEM((half_rows, cols2, chan), BF16),
                pltpu.VMEM((chan, chan), BF16),
                dma((2, 4, line)),
                dma((2, 2, line)),
                dma((2, line)),
                dma((2, 2, line)),
                dma((chips,)),
                dma((chips,)),
                dma((4,)),
                dma((4,)),
            ],
            compiler_params=pltpu.CompilerParams(
                collective_id=0, has_side_effects=True, vmem_limit_bytes=48 * 1024 * 1024
            ),
            cost_estimate=pl.CostEstimate(flops=3 * 10**9, bytes_accessed=10**6, transcendentals=2 * 10**6),
        )(pair, w_query, w_kv, w_gate, w_out, pair_bias, lengths)

    in_specs = (P("grp", "col", None), P(), P(), P(), P(), P("grp", "col", None), P("grp"))
    return jax.shard_map(
        on_device, mesh=mesh, in_specs=in_specs, out_specs=P("grp", "col", None), check_vma=False
    )
```

time: 115 us -> 46.7 us (0.41)
  waiting for transfers between devices: 52.3 us -> 0 us
  Pallas kernels: 0 us -> 40 us
  matrix products: 21.1 us -> 0 us
  between operations: 13.5 us -> 0.67 us
  other arithmetic: 8.07 us -> 0 us
  starting transfers between devices: 7.3 us -> 0 us
  local copies, waits for them, and re-layouts: 11.1 us -> 5.62 us
  loops' own time: 1.31 us -> 0 us
    all_gather x1 -> x0, waiting for transfers between devices: 43.4 us -> none  [gather_keys(): lax.all_gather(normed, 'col', axis=1, tiled=True)]
    pallas_call x0 -> x1, Pallas kernels: none -> 40 us  [on_device(): pl.pallas_call(functools.partial(body, line), out_shape=jax.ShapeDtypeStr...]
    dot_general x8 -> x0, matrix products: 21.1 us -> none  [the longest x2 6.84 us: consume(): jnp.einsum('rhjk,rkhd->rjhd', weights, value_tile, preferred_element_type...]
    all_to_all x1 -> x0, waiting for transfers between devices: 8.85 us -> none  [on_device(): lax.all_to_all(pair_bias, 'col', split_axis=2, concat_axis=1, tiled=True)]
    all_to_all x1 -> x0, starting transfers between devices: 7.3 us -> none  [on_device(): lax.all_to_all(pair_bias, 'col', split_axis=2, concat_axis=1, tiled=True)]
    reduce_sum x4 -> x0, other arithmetic: 4.61 us -> none  [the longest x2 2.38 us: consume(): new_sum = run_sum * rescale + jnp.sum(expon, axis=-1)]
    convert_element_type x3 -> x0, other arithmetic: 1.81 us -> none  [the longest x1 1.76 us: normalize(): return (centred * lax.rsqrt(variance + 1e-05)).astype(jnp.bfloat16)]
    all_to_all x2 -> x0, local copies, waits for them, and re-layouts: 1.77 us -> none  [on_device(): lax.all_to_all(pair_bias, 'col', split_axis=2, concat_axis=1, tiled=True)]
  transfers between devices with their start and end apart: 2 -> 0, of which waited for: 2 -> 0; matrix products, arithmetic and copies ran while one was open for 7% -> 0% of each run, Pallas kernels for 0% -> 0%
where the time goes in v1:
time: 46.7 us; the launch traced here: 46.3 us
  Pallas kernels  40 us (86%)
  local copies, waits for them, and re-layouts  5.62 us (12%)
  between operations  0.67 us (1%)
    pallas_call x1, Pallas kernels, on_device(): pl.pallas_call(functools.partial(body, line), out_shape=jax.ShapeDtypeStr...  40 us
    unnamed x13, local copies, waits for them, and re-layouts  5.62 us

profile of v1, /device:TPU:0, one launch (start us, length us, event | category | flops | bytes accessed | tf_op | source)
XLA Modules:
  0.0 46.3 jit_solution(16564277967451217180)
XLA Ops:
  0.7 0.0 copy-start
  0.7 0.9 %copy-done = bf16[4,32,1024]{2,1,0:T(8,128)(2,1)S(1)} copy-done((bf16[4,32,1024]{2,1,0:T(8,128)(2,1)S(1)}, bf16[4,32,1024]{2,1,0:T(8,128)(2,1)}, u32[]{:S(2)}) %copy-start) | copy-done | bytes 262168
  1.6 0.0 copy-start.1
  1.6 0.9 %copy-done.1 = bf16[16,32,128]{2,1,0:T(8,128)(2,1)S(1)} copy-done((bf16[16,32,128]{2,1,0:T(8,128)(2,1)S(1)}, bf16[16,32,128]{2,1,0:T(8,128)(2,1)}, u32[]{:S(2)}) %copy-start.1) | copy-done | bytes 131096
  2.5 0.0 copy-start.2
  2.5 0.8 %copy-done.2 = bf16[128,256]{1,0:T(8,128)(2,1)S(1)} copy-done((bf16[128,256]{1,0:T(8,128)(2,1)S(1)}, bf16[128,256]{1,0:T(8,128)(2,1)}, u32[]{:S(2)}) %copy-start.2) | copy-done | bytes 65560
  3.3 0.0 copy-start.3
  3.4 0.8 %copy-done.3 = bf16[128,128]{1,0:T(8,128)(2,1)S(1)} copy-done((bf16[128,128]{1,0:T(8,128)(2,1)S(1)}, bf16[128,128]{1,0:T(8,128)(2,1)}, u32[]{:S(2)}) %copy-start.3) | copy-done | bytes 32792
  4.1 0.0 copy-start.4
  4.1 0.8 %copy-done.4 = bf16[128,128]{1,0:T(8,128)(2,1)S(1)} copy-done((bf16[128,128]{1,0:T(8,128)(2,1)S(1)}, bf16[128,128]{1,0:T(8,128)(2,1)}, u32[]{:S(2)}) %copy-start.4) | copy-done | bytes 32792
  4.9 0.0 copy-start.5
  4.9 0.8 %copy-done.5 = bf16[128,128]{1,0:T(8,128)(2,1)S(1)} copy-done((bf16[128,128]{1,0:T(8,128)(2,1)S(1)}, bf16[128,128]{1,0:T(8,128)(2,1)}, u32[]{:S(2)}) %copy-start.5) | copy-done | bytes 32792
  5.6 40.0 %shard_map.73 = bf16[16,32,128]{2,1,0:T(8,128)(2,1)S(1)} custom-call(bf16[16,32,128]{2,1,0:T(8,128)(2,1)S(1)} %copy-done.1, bf16[128,128]{1,0:T(8,128)(2,1)S(1)} %copy-done.3, bf16[128,256]{1,0:T(8,128)(2,1)S(1)} %copy-done.2, bf16[128,128]{1,0:T(8,128)(2,1)S(1)} %copy-done.4, bf16[128,128]{1,0:T(8,128)(2,1)S(1)} %copy-done.5, ...), custom_call_target="tpu_custom_call" | custom-call | flops 3000000000 | bytes 1000000 | tf_op jit(solution)/shard_map/pallas_call | solution.py:339
  45.6 0.7 %copy.10 = bf16[16,32,128]{2,1,0:T(8,128)(2,1)} copy(bf16[16,32,128]{2,1,0:T(8,128)(2,1)S(1)} %shard_map.73) | data formatting | bytes 262144
Async XLA Ops:
  0.7 1.0 %copy-start = (bf16[4,32,1024]{2,1,0:T(8,128)(2,1)S(1)}, bf16[4,32,1024]{2,1,0:T(8,128)(2,1)}, u32[]{:S(2)}) copy-start(bf16[4,32,1024]{2,1,0:T(8,128)(2,1)} %bias_ref.1) | copy-start | bytes 786436
  1.6 0.9 %copy-start.1 = (bf16[16,32,128]{2,1,0:T(8,128)(2,1)S(1)}, bf16[16,32,128]{2,1,0:T(8,128)(2,1)}, u32[]{:S(2)}) copy-start(bf16[16,32,128]{2,1,0:T(8,128)(2,1)} %pair_ref.1) | copy-start | bytes 393220
  2.5 0.8 %copy-start.2 = (bf16[128,256]{1,0:T(8,128)(2,1)S(1)}, bf16[128,256]{1,0:T(8,128)(2,1)}, u32[]{:S(2)}) copy-start(bf16[128,256]{1,0:T(8,128)(2,1)} %wkv_ref.1) | copy-start | bytes 196612
  3.3 0.8 %copy-start.3 = (bf16[128,128]{1,0:T(8,128)(2,1)S(1)}, bf16[128,128]{1,0:T(8,128)(2,1)}, u32[]{:S(2)}) copy-start(bf16[128,128]{1,0:T(8,128)(2,1)} %wq_ref.1) | copy-start | bytes 98308
  4.1 0.8 %copy-start.4 = (bf16[128,128]{1,0:T(8,128)(2,1)S(1)}, bf16[128,128]{1,0:T(8,128)(2,1)}, u32[]{:S(2)}) copy-start(bf16[128,128]{1,0:T(8,128)(2,1)} %wg_ref.1) | copy-start | bytes 98308
  4.9 0.8 %copy-start.5 = (bf16[128,128]{1,0:T(8,128)(2,1)S(1)}, bf16[128,128]{1,0:T(8,128)(2,1)}, u32[]{:S(2)}) copy-start(bf16[128,128]{1,0:T(8,128)(2,1)} %wo_ref.1) | copy-start | bytes 98308

commit v2 on v1

--- a/solution.py
+++ b/solution.py
@@ -29,7 +29,8 @@
 
 
 def body(
-    line, pair_ref, wq_ref, wkv_ref, wg_ref, wo_ref, bias_ref, len_ref, out_ref,
+    line, pair_in, wq_in, wkv_in, wg_in, wo_in, bias_in, len_ref, out_ref,
+    pair_ref, bias_ref, wq_ref, wkv_ref, wg_ref, wo_ref, load_sem,
     gath, swap, bsend, bgath, bias_f, amat, gate, acc, run_max, run_sum, upd,
     wvt_ref, recv, zsend, nsend, fsend, bs_sem, br_sem, core_s, core_r,
 ):
@@ -55,6 +56,16 @@
     def device(z_at, xy_at):
         return {"col": (z_at * 4 + xy_at) * 2 + core}
 
+    loads = [
+        pltpu.make_async_copy(source, target, load_sem.at[at])
+        for at, (source, target) in enumerate((
+            (pair_in, pair_ref), (bias_in, bias_ref), (wq_in, wq_ref),
+            (wkv_in, wkv_ref), (wg_in, wg_ref), (wo_in, wo_ref),
+        ))
+    ]
+    for load in loads:
+        load.start()
+
     barrier = pltpu.get_barrier_semaphore()
 
     def greet(k, carry):
@@ -71,6 +82,7 @@
         variance = jnp.mean(centred * centred, axis=-1, keepdims=True)
         return (centred * lax.rsqrt(variance + 1e-05)).astype(BF16)
 
+    loads[0].wait()
     own_cols = pl.ds(pl.multiple_of(core * cols, cols), cols)
     swap[...] = normalized((1 - core) * half_rows)
     gath[xy, z, :, own_cols, :] = normalized(core * half_rows)
@@ -84,6 +96,7 @@
     )
     swap_copy.start()
 
+    loads[1].wait()
     low = lax.broadcasted_iota(jnp.int32, (cols, 2 * cols2), 1) < cols2
     for pair_at in range(chips // 2):
         parts = [
@@ -141,6 +154,8 @@
     lax.fori_loop(1, chips, send_bias, 0)
     bgath[xy, z, own_cols, :] = bsend[chip]
 
+    for load in loads[2:]:
+        load.wait()
     wqt = transposed(wq_ref[...])
     wgt = transposed(wg_ref[...])
     wvt_ref[...] = transposed(wkv_ref[:, chan:])
@@ -339,9 +354,16 @@
         return pl.pallas_call(
             functools.partial(body, line),
             out_shape=jax.ShapeDtypeStruct(pair.shape, BF16),
-            in_specs=[vmem] * 6 + [pl.BlockSpec(memory_space=pltpu.SMEM)],
+            in_specs=[pl.BlockSpec(memory_space=pltpu.HBM)] * 6 + [pl.BlockSpec(memory_space=pltpu.SMEM)],
             out_specs=vmem,
             scratch_shapes=[
+                pltpu.VMEM(pair.shape, BF16),
+                pltpu.VMEM(pair_bias.shape, BF16),
+                pltpu.VMEM(w_query.shape, BF16),
+                pltpu.VMEM(w_kv.shape, BF16),
+                pltpu.VMEM(w_gate.shape, BF16),
+                pltpu.VMEM(w_out.shape, BF16),
+                dma((6,)),
                 pltpu.VMEM((4, line, half_rows, cols2, chan), BF16),
                 pltpu.VMEM((half_rows, cols, chan), BF16),
                 pltpu.VMEM((chips, cols, lanes), BF16),

time: 46.7 us -> 47.2 us (1.011)
  Pallas kernels: 40 us -> 40.5 us
    pallas_call x1, Pallas kernels: 40 us -> 40.5 us  [on_device(): pl.pallas_call(functools.partial(body, line), out_shape=jax.ShapeDtypeStr...]
where the time goes in v2:
time: 47.2 us; the launch traced here: 46.8 us
  Pallas kernels  40.5 us (86%)
  local copies, waits for them, and re-layouts  5.62 us (12%)
  between operations  0.67 us (1%)
    pallas_call x1, Pallas kernels, on_device(): pl.pallas_call(functools.partial(body, line), out_shape=jax.ShapeDtypeStr...  40.5 us
    unnamed x13, local copies, waits for them, and re-layouts  5.62 us

profile of v2, /device:TPU:0, one launch (start us, length us, event | category | flops | bytes accessed | tf_op | source)
XLA Modules:
  0.0 46.8 jit_solution(16491718102794211201)
XLA Ops:
  0.7 0.0 copy-start
  0.7 0.9 %copy-done = bf16[4,32,1024]{2,1,0:T(8,128)(2,1)S(1)} copy-done((bf16[4,32,1024]{2,1,0:T(8,128)(2,1)S(1)}, bf16[4,32,1024]{2,1,0:T(8,128)(2,1)}, u32[]{:S(2)}) %copy-start) | copy-done | bytes 262168
  1.6 0.0 copy-start.1
  1.6 0.9 %copy-done.1 = bf16[16,32,128]{2,1,0:T(8,128)(2,1)S(1)} copy-done((bf16[16,32,128]{2,1,0:T(8,128)(2,1)S(1)}, bf16[16,32,128]{2,1,0:T(8,128)(2,1)}, u32[]{:S(2)}) %copy-start.1) | copy-done | bytes 131096
  2.5 0.0 copy-start.2
  2.5 0.8 %copy-done.2 = bf16[128,256]{1,0:T(8,128)(2,1)S(1)} copy-done((bf16[128,256]{1,0:T(8,128)(2,1)S(1)}, bf16[128,256]{1,0:T(8,128)(2,1)}, u32[]{:S(2)}) %copy-start.2) | copy-done | bytes 65560
  3.3 0.0 copy-start.3
  3.4 0.8 %copy-done.3 = bf16[128,128]{1,0:T(8,128)(2,1)S(1)} copy-done((bf16[128,128]{1,0:T(8,128)(2,1)S(1)}, bf16[128,128]{1,0:T(8,128)(2,1)}, u32[]{:S(2)}) %copy-start.3) | copy-done | bytes 32792
  4.1 0.0 copy-start.4
  4.1 0.8 %copy-done.4 = bf16[128,128]{1,0:T(8,128)(2,1)S(1)} copy-done((bf16[128,128]{1,0:T(8,128)(2,1)S(1)}, bf16[128,128]{1,0:T(8,128)(2,1)}, u32[]{:S(2)}) %copy-start.4) | copy-done | bytes 32792
  4.9 0.0 copy-start.5
  4.9 0.8 %copy-done.5 = bf16[128,128]{1,0:T(8,128)(2,1)S(1)} copy-done((bf16[128,128]{1,0:T(8,128)(2,1)S(1)}, bf16[128,128]{1,0:T(8,128)(2,1)}, u32[]{:S(2)}) %copy-start.5) | copy-done | bytes 32792
  5.6 40.5 %shard_map.73 = bf16[16,32,128]{2,1,0:T(8,128)(2,1)S(1)} custom-call(bf16[16,32,128]{2,1,0:T(8,128)(2,1)S(1)} %copy-done.1, bf16[128,128]{1,0:T(8,128)(2,1)S(1)} %copy-done.3, bf16[128,256]{1,0:T(8,128)(2,1)S(1)} %copy-done.2, bf16[128,128]{1,0:T(8,128)(2,1)S(1)} %copy-done.4, bf16[128,128]{1,0:T(8,128)(2,1)S(1)} %copy-done.5, ...), custom_call_target="tpu_custom_call" | custom-call | flops 3000000000 | bytes 1000000 | tf_op jit(solution)/shard_map/pallas_call | solution.py:354
  46.2 0.7 %copy.10 = bf16[16,32,128]{2,1,0:T(8,128)(2,1)} copy(bf16[16,32,128]{2,1,0:T(8,128)(2,1)S(1)} %shard_map.73) | data formatting | bytes 262144
Async XLA Ops:
  0.7 1.0 %copy-start = (bf16[4,32,1024]{2,1,0:T(8,128)(2,1)S(1)}, bf16[4,32,1024]{2,1,0:T(8,128)(2,1)}, u32[]{:S(2)}) copy-start(bf16[4,32,1024]{2,1,0:T(8,128)(2,1)} %bias_in.1) | copy-start | bytes 786436
  1.6 0.9 %copy-start.1 = (bf16[16,32,128]{2,1,0:T(8,128)(2,1)S(1)}, bf16[16,32,128]{2,1,0:T(8,128)(2,1)}, u32[]{:S(2)}) copy-start(bf16[16,32,128]{2,1,0:T(8,128)(2,1)} %pair_in.1) | copy-start | bytes 393220
  2.5 0.8 %copy-start.2 = (bf16[128,256]{1,0:T(8,128)(2,1)S(1)}, bf16[128,256]{1,0:T(8,128)(2,1)}, u32[]{:S(2)}) copy-start(bf16[128,256]{1,0:T(8,128)(2,1)} %wkv_in.1) | copy-start | bytes 196612
  3.3 0.8 %copy-start.3 = (bf16[128,128]{1,0:T(8,128)(2,1)S(1)}, bf16[128,128]{1,0:T(8,128)(2,1)}, u32[]{:S(2)}) copy-start(bf16[128,128]{1,0:T(8,128)(2,1)} %wq_in.1) | copy-start | bytes 98308
  4.1 0.8 %copy-start.4 = (bf16[128,128]{1,0:T(8,128)(2,1)S(1)}, bf16[128,128]{1,0:T(8,128)(2,1)}, u32[]{:S(2)}) copy-start(bf16[128,128]{1,0:T(8,128)(2,1)} %wg_in.1) | copy-start | bytes 98308
  4.9 0.8 %copy-start.5 = (bf16[128,128]{1,0:T(8,128)(2,1)S(1)}, bf16[128,128]{1,0:T(8,128)(2,1)}, u32[]{:S(2)}) copy-start(bf16[128,128]{1,0:T(8,128)(2,1)} %wo_in.1) | copy-start | bytes 98308

commit v3 on v2

--- a/solution.py
+++ b/solution.py
@@ -31,7 +31,7 @@
 def body(
     line, pair_in, wq_in, wkv_in, wg_in, wo_in, bias_in, len_ref, out_ref,
     pair_ref, bias_ref, wq_ref, wkv_ref, wg_ref, wo_ref, load_sem,
-    gath, swap, bsend, bgath, bias_f, amat, gate, acc, run_max, run_sum, upd,
+    gath, swap, bsend, bgath, bias_f, queries, gate, acc, run_max, run_sum, upd,
     wvt_ref, recv, zsend, nsend, fsend, bs_sem, br_sem, core_s, core_r,
 ):
     rows, cols, chan = pair_ref.shape
@@ -159,7 +159,6 @@
     wqt = transposed(wq_ref[...])
     wgt = transposed(wg_ref[...])
     wvt_ref[...] = transposed(wkv_ref[:, chan:])
-    w_key = wkv_ref[:, :chan]
     same_head = (
         lax.broadcasted_iota(jnp.int32, (chan, lanes), 0) // width
         == lax.broadcasted_iota(jnp.int32, (chan, lanes), 1) // cols2
@@ -168,9 +167,9 @@
     def prepare(r, carry):
         own = gath[xy, z, r]
         repeated = jnp.concatenate([own] * HEADS, axis=0)
-        queries = (dot_nt(wqt, repeated) * width ** (-0.5)).astype(BF16).astype(F32)
-        queries = jnp.where(same_head, queries, 0.0).astype(BF16)
-        amat[r] = (dot(w_key, queries) * LOG2E).astype(BF16)
+        own_query = (dot_nt(wqt, repeated) * width ** (-0.5)).astype(BF16).astype(F32)
+        own_query = jnp.where(same_head, own_query, 0.0).astype(BF16)
+        queries[r] = own_query
         gate[r] = jax.nn.sigmoid(dot_nt(wgt, own))
         return carry
 
@@ -247,36 +246,43 @@
     acc[...] = jnp.zeros_like(acc)
     group = 4 if line % 4 == 0 else 1
     keys = group * cols2
+    row_step = 2
 
     def fold(half, lines):
         wvt = wvt_ref[...]
-
-        def one(step, carry):
-            r = half * quarter + step // (line // group)
-            z_at = pl.ds(lax.rem(step, line // group) * group, group)
-            tiles = [gath[at, z_at, r].reshape(keys, chan) for at in lines]
-            scores = [
-                dot(tile, amat[r]) + bias_f[at, z_at].reshape(keys, lanes)
-                for tile, at in zip(tiles, lines)
-            ]
-            old_max = run_max[r]
-            new_max = old_max
-            for part in scores:
-                new_max = jnp.maximum(new_max, jnp.max(part, axis=0, keepdims=True))
-            rescale = jnp.exp2(old_max - new_max)
-            total = run_sum[r] * rescale
-            result = acc[r] * rescale
-            for part, tile in zip(scores, tiles):
-                expon = jnp.exp2(part - new_max)
-                total = total + jnp.sum(expon, axis=0, keepdims=True)
-                result = result + dot(dot_nt(wvt, tile).astype(BF16), expon.astype(BF16))
-            run_max[r] = new_max
-            run_sum[r] = total
-            acc[r] = result
-            return carry
-
-        steps = quarter * (line // group)
-        lax.fori_loop(0, steps, one, 0, unroll=2)
+        w_key = wkv_ref[:, :chan]
+
+        def one_group(rows_at, part_at):
+            z_at = pl.ds(part_at * group, group)
+            olds = [(run_max[r], run_sum[r], acc[r]) for r in rows_at]
+            news = []
+            for r, (old_max, old_sum, old_acc) in zip(rows_at, olds):
+                tiles = [gath[at, z_at, r].reshape(keys, chan) for at in lines]
+                scores = [
+                    dot(dot(tile, w_key).astype(BF16), queries[r]) * LOG2E
+                    + bias_f[at, z_at].reshape(keys, lanes)
+                    for tile, at in zip(tiles, lines)
+                ]
+                new_max = old_max
+                for part in scores:
+                    new_max = jnp.maximum(new_max, jnp.max(part, axis=0, keepdims=True))
+                rescale = jnp.exp2(old_max - new_max)
+                total = old_sum * rescale
+                result = old_acc * rescale
+                for part, tile in zip(scores, tiles):
+                    expon = jnp.exp2(part - new_max)
+                    total = total + jnp.sum(expon, axis=0, keepdims=True)
+                    result = result + dot(dot_nt(wvt, tile).astype(BF16), expon.astype(BF16))
+                news.append((new_max, total, result))
+            for r, new in zip(rows_at, news):
+                run_max[r], run_sum[r], acc[r] = new
+
+        for first in range(half * quarter, (half + 1) * quarter, row_step):
+            rows_at = range(first, first + row_step)
+            if line == group:
+                one_group(rows_at, 0)
+            else:
+                lax.fori_loop(0, line // group, lambda at, _: one_group(rows_at, at), None)
 
     def wait_line(half, at):
         for z_at in range(line):
@@ -302,21 +308,20 @@
         wait_line(half, diag)
         fold(half, (diag,))
 
-        def finish(step, carry):
-            r = half * quarter + step
-            result = acc[r] / run_sum[r]
+        hiddens = []
+        for r in range(half * quarter, (half + 1) * quarter):
+            result = acc[r] * (1.0 / run_sum[r])
             parts = []
             for h in range(HEADS):
-                block = result[h * width : (h + 1) * width, (h // 2) * 2 * cols2 : (h // 2 + 1) * 2 * cols2]
+                pair_of = slice((h // 2) * 2 * cols2, (h // 2 + 1) * 2 * cols2)
+                block = result[h * width : (h + 1) * width, pair_of]
                 if h % 2:
                     block = pltpu.roll(block, cols2, 1)
                 parts.append(block[:, :cols2])
             attended = jnp.concatenate(parts, axis=0)
-            hidden = (gate[r] * attended).T.astype(BF16)
-            upd[r] = dot(hidden, wo_ref[...]).astype(BF16)
-            return carry
-
-        lax.fori_loop(0, quarter, finish, 0, unroll=2)
+            hiddens.append((gate[r] * attended).T.astype(BF16))
+        update = dot(jnp.concatenate(hiddens, axis=0), wo_ref[...]).astype(BF16)
+        upd[pl.ds(half * quarter, quarter)] = update.reshape(quarter, cols2, chan)
         out_copy(half).start()
         out_ref[pl.ds(core * half_rows + half * quarter, quarter)] = upd[
             pl.ds(half * quarter, quarter), own_cols, :
@@ -354,7 +359,7 @@
         return pl.pallas_call(
             functools.partial(body, line),
             out_shape=jax.ShapeDtypeStruct(pair.shape, BF16),
-            in_specs=[pl.BlockSpec(memory_space=pltpu.HBM)] * 6 + [pl.BlockSpec(memory_space=pltpu.SMEM)],
+            in_specs=[pl.BlockSpec(memory_space=pl.ANY)] * 6 + [pl.BlockSpec(memory_space=pltpu.SMEM)],
             out_specs=vmem,
             scratch_shapes=[
                 pltpu.VMEM(pair.shape, BF16),
@@ -386,7 +391,7 @@
                 dma((4,)),
             ],
             compiler_params=pltpu.CompilerParams(
-                collective_id=0, has_side_effects=True, vmem_limit_bytes=48 * 1024 * 1024
+                collective_id=0, has_side_effects=True
             ),
             cost_estimate=pl.CostEstimate(flops=3 * 10**9, bytes_accessed=10**6, transcendentals=2 * 10**6),
         )(pair, w_query, w_kv, w_gate, w_out, pair_bias, lengths)

time: 47.2 us -> 43.3 us (0.917)
  local copies, waits for them, and re-layouts: 5.62 us -> 1.57 us
  Pallas kernels: 40.5 us -> 41 us
    unnamed x13 -> x1, local copies, waits for them, and re-layouts: 5.62 us -> 1.57 us
where the time goes in v3:
time: 43.3 us; the launch traced here: 43.2 us
  Pallas kernels  41 us (95%)
  local copies, waits for them, and re-layouts  1.57 us (4%)
  between operations  0.66 us (2%)
    pallas_call x1, Pallas kernels, on_device(): pl.pallas_call(functools.partial(body, line), out_shape=jax.ShapeDtypeStr...  41 us
    unnamed x1, local copies, waits for them, and re-layouts  1.57 us

profile of v3, /device:TPU:0, one launch (start us, length us, event | category | flops | bytes accessed | tf_op | source)
XLA Modules:
  0.0 43.2 jit_solution(16328464981502339466)
XLA Ops:
  0.7 41.0 %shard_map.73 = bf16[16,32,128]{2,1,0:T(8,128)(2,1)} custom-call(bf16[16,32,128]{2,1,0:T(8,128)(2,1)} %pair_in.1, bf16[128,128]{1,0:T(8,128)(2,1)} %wq_in.1, bf16[128,256]{1,0:T(8,128)(2,1)} %wkv_in.1, bf16[128,128]{1,0:T(8,128)(2,1)} %wg_in.1, bf16[128,128]{1,0:T(8,128)(2,1)} %wo_in.1, bf16[4,32,1024]{2,1,0:T(8,128)(2,1)} %bias_in.1, s32[1]{0:T(128)S(6)} %copy.9.len_ref), custom_call_target="tpu_custom_call" | custom-call | flops 3000000000 | bytes 1000000 | tf_op jit(solution)/shard_map/pallas_call | solution.py:359
  41.6 1.6 %copy.10 = bf16[16,32,128]{2,1,0:T(8,128)(2,1)} copy(bf16[16,32,128]{2,1,0:T(8,128)(2,1)} %shard_map.73) | data formatting | bytes 262144

commit v4 on v3

--- a/solution.py
+++ b/solution.py
@@ -147,11 +147,16 @@
             device_id={"col": other * 2 + core}, device_id_type=MESH,
         )
 
-    def send_bias(k, carry):
-        bias_copy(lax.rem(chip + k, chips), chip).start()
-        return carry
-
-    lax.fori_loop(1, chips, send_bias, 0)
+    def bias_peers(line_at, first, act):
+        def one(k, carry):
+            act(lax.rem(z + k, line) * 4 + line_at)
+            return carry
+
+        lax.fori_loop(first, line, one, 0)
+
+    all_lines = ((xy, 1), (x_line, 0), (y_line, 0), (diag, 0))
+    for line_at, first in all_lines:
+        bias_peers(line_at, first, lambda other: bias_copy(other, chip).start())
     bgath[xy, z, own_cols, :] = bsend[chip]
 
     for load in loads[2:]:
@@ -210,89 +215,113 @@
         if s:
             pl.when(z + s < line)(upper)
 
-    for s in range(1, line):
-        pass_line(s)
-        pass_near(s - 1)
-    pass_near(line - 1)
-
-    def wait_bias(k, carry):
-        other = lax.rem(chip + k, chips)
-        bias_copy(other, other).wait_recv()
-        return carry
-
-    lax.fori_loop(1, chips, wait_bias, 0)
-    bias_swap = pltpu.make_async_remote_copy(
-        src_ref=bgath.at[:, :, own_cols, :], dst_ref=bgath.at[:, :, own_cols, :],
-        send_sem=core_s.at[1], recv_sem=core_r.at[1],
-        device_id={"col": sibling}, device_id_type=MESH,
-    )
-    bias_swap.start()
-    bias_swap.wait_recv()
+    def bias_swap(at):
+        line_at = all_lines[at][0]
+        return pltpu.make_async_remote_copy(
+            src_ref=bgath.at[line_at, :, own_cols, :], dst_ref=bgath.at[line_at, :, own_cols, :],
+            send_sem=core_s.at[3 + at], recv_sem=core_r.at[3 + at],
+            device_id={"col": sibling}, device_id_type=MESH,
+        )
+
+    def start_bias(at):
+        line_at, first = all_lines[at]
+        bias_peers(line_at, first, lambda other: bias_copy(other, other).wait_recv())
+        bias_swap(at).start()
 
     limit = len_ref[0]
 
-    def spread_bias(k, carry):
-        line_at, z_at = k // line, lax.rem(k, line)
-        first = (z_at * 4 + line_at) * cols2
-        position = first + lax.broadcasted_iota(jnp.int32, (cols2, lanes), 0)
-        mask = jnp.where(position < limit, 0.0, -1000000000.0)
-        bias_f[line_at, z_at] = (bgath[line_at, z_at].astype(F32) + mask) * LOG2E
-        return carry
-
-    lax.fori_loop(0, chips, spread_bias, 0)
+    def spread_bias(at):
+        bias_swap(at).wait_recv()
+        line_at = all_lines[at][0]
+
+        def one(z_at, carry):
+            first = (z_at * 4 + line_at) * cols2
+            position = first + lax.broadcasted_iota(jnp.int32, (cols2, lanes), 0)
+            mask = jnp.where(position < limit, 0.0, -1000000000.0)
+            bias_f[line_at, z_at] = (bgath[line_at, z_at].astype(F32) + mask) * LOG2E
+            return carry
+
+        lax.fori_loop(0, line, one, 0)
 
     run_max[...] = jnp.full_like(run_max, -1e30)
     run_sum[...] = jnp.zeros_like(run_sum)
     acc[...] = jnp.zeros_like(acc)
-    group = 4 if line % 4 == 0 else 1
+    group = line // 2
     keys = group * cols2
-    row_step = 2
-
-    def fold(half, lines):
-        wvt = wvt_ref[...]
-        w_key = wkv_ref[:, :chan]
-
-        def one_group(rows_at, part_at):
-            z_at = pl.ds(part_at * group, group)
-            olds = [(run_max[r], run_sum[r], acc[r]) for r in rows_at]
-            news = []
-            for r, (old_max, old_sum, old_acc) in zip(rows_at, olds):
-                tiles = [gath[at, z_at, r].reshape(keys, chan) for at in lines]
-                scores = [
-                    dot(dot(tile, w_key).astype(BF16), queries[r]) * LOG2E
-                    + bias_f[at, z_at].reshape(keys, lanes)
-                    for tile, at in zip(tiles, lines)
-                ]
-                new_max = old_max
-                for part in scores:
-                    new_max = jnp.maximum(new_max, jnp.max(part, axis=0, keepdims=True))
-                rescale = jnp.exp2(old_max - new_max)
-                total = old_sum * rescale
-                result = old_acc * rescale
-                for part, tile in zip(scores, tiles):
-                    expon = jnp.exp2(part - new_max)
-                    total = total + jnp.sum(expon, axis=0, keepdims=True)
-                    result = result + dot(dot_nt(wvt, tile).astype(BF16), expon.astype(BF16))
-                news.append((new_max, total, result))
-            for r, new in zip(rows_at, news):
-                run_max[r], run_sum[r], acc[r] = new
-
-        for first in range(half * quarter, (half + 1) * quarter, row_step):
-            rows_at = range(first, first + row_step)
-            if line == group:
-                one_group(rows_at, 0)
-            else:
-                lax.fori_loop(0, line // group, lambda at, _: one_group(rows_at, at), None)
-
-    def wait_line(half, at):
-        for z_at in range(line):
-            arrived(half, at, z_at)
-
-    for half in range(2):
-        fold(half, (xy, near[half]))
-    for half in range(2):
-        wait_line(half, far[half])
-        fold(half, (far[half],))
+    own_part = z // group
+    per_pair = 2 * cols2
+
+    def fold(half, line_at, part):
+        first = half * quarter
+        z_at = pl.ds(part * group, group)
+        tiles = [gath[line_at, z_at, first + r].reshape(keys, chan) for r in range(quarter)]
+        olds = [(run_max[first + r], run_sum[first + r], acc[first + r]) for r in range(quarter)]
+        bias_tile = bias_f[line_at, z_at].reshape(keys, lanes)
+        together = jnp.concatenate(tiles, axis=0)
+        all_keys = dot(together, wkv_ref[:, :chan]).astype(BF16)
+        all_values = dot_nt(wvt_ref[...], together).astype(BF16)
+        news = []
+        for r, (old_max, old_sum, old_acc) in enumerate(olds):
+            span = slice(r * keys, (r + 1) * keys)
+            scores = dot(all_keys[span], queries[first + r]) * LOG2E + bias_tile
+            new_max = jnp.maximum(old_max, jnp.max(scores, axis=0, keepdims=True))
+            rescale = jnp.exp2(old_max - new_max)
+            expon = jnp.exp2(scores - new_max)
+            total = old_sum * rescale + jnp.sum(expon, axis=0, keepdims=True)
+            product = dot(all_values[:, span], expon.astype(BF16))
+            result = []
+            for h in range(HEADS):
+                at = slice(h * width, (h + 1) * width)
+                pair_of = slice((h // 2) * per_pair, (h // 2 + 1) * per_pair)
+                result.append(old_acc[at] * rescale[:, pair_of] + product[at, pair_of])
+            news.append((new_max, total, jnp.concatenate(result, axis=0)))
+        for r, new in enumerate(news):
+            run_max[first + r], run_sum[first + r], acc[first + r] = new
+
+    def pick(half, lines):
+        return jnp.where(half == 0, lines[0], lines[1])
+
+    def fold_both(lines, part):
+        def one(half, carry):
+            fold(half, pick(half, lines), part)
+            return carry
+
+        lax.fori_loop(0, 2, one, 0)
+
+    own = (xy, xy)
+    for s in range(1, line):
+        pass_line(s)
+        if s == group - 1 or line == 2:
+            start_bias(0)
+            pass_near(s - 1)
+            spread_bias(0)
+            fold_both(own, own_part)
+        elif s == line - 2:
+            start_bias(1)
+            start_bias(2)
+            pass_near(s - 1)
+            spread_bias(1)
+            spread_bias(2)
+            fold_both(near, own_part)
+        else:
+            pass_near(s - 1)
+    start_bias(3)
+    fold_both(own, 1 - own_part)
+    pass_near(line - 1)
+    spread_bias(3)
+    fold_both(near, 1 - own_part)
+
+    def late(unit, carry):
+        half, stage = lax.rem(unit, 2), unit // 2
+        line_at = jnp.where(stage < 2, pick(half, far), diag)
+        part = jnp.where(lax.rem(stage, 2) == 0, own_part, 1 - own_part)
+        for z_at in range(group):
+            block = gath.at[line_at, part * group + z_at, pl.ds(half * quarter, quarter)]
+            pltpu.make_async_copy(block, block, recv.at[half, line_at, part * group + z_at]).wait()
+        fold(half, line_at, part)
+        return carry
+
+    lax.fori_loop(0, 7, late, 0)
 
     other_cols = pl.ds(pl.multiple_of((1 - core) * cols, cols), cols)
 
@@ -300,21 +329,19 @@
         return pltpu.make_async_remote_copy(
             src_ref=upd.at[pl.ds(half * quarter, quarter), other_cols, :],
             dst_ref=out_ref.at[pl.ds(core * half_rows + half * quarter, quarter)],
-            send_sem=core_s.at[2 + half], recv_sem=core_r.at[2 + half],
+            send_sem=core_s.at[1 + half], recv_sem=core_r.at[1 + half],
             device_id={"col": sibling}, device_id_type=MESH,
         )
 
     for half in range(2):
-        wait_line(half, diag)
-        fold(half, (diag,))
-
+        if half:
+            late(7, 0)
         hiddens = []
         for r in range(half * quarter, (half + 1) * quarter):
-            result = acc[r] * (1.0 / run_sum[r])
+            scale = 1.0 / run_sum[r]
             parts = []
             for h in range(HEADS):
-                pair_of = slice((h // 2) * 2 * cols2, (h // 2 + 1) * 2 * cols2)
-                block = result[h * width : (h + 1) * width, pair_of]
+                block = acc[r, h * width : (h + 1) * width] * scale[:, (h // 2) * per_pair : (h // 2 + 1) * per_pair]
                 if h % 2:
                     block = pltpu.roll(block, cols2, 1)
                 parts.append(block[:, :cols2])
@@ -336,13 +363,9 @@
             to_far(half, 0, z_at).wait_send()
             to_far(half, 1, z_at).wait_send()
     swap_copy.wait_send()
-    bias_swap.wait_send()
-
-    def drain_bias(k, carry):
-        bias_copy(lax.rem(chip + k, chips), chip).wait_send()
-        return carry
-
-    lax.fori_loop(1, chips, drain_bias, 0)
+    for at, (line_at, first) in enumerate(all_lines):
+        bias_peers(line_at, first, lambda other: bias_copy(other, chip).wait_send())
+        bias_swap(at).wait_send()
 
 
 def solution(mesh):
@@ -376,7 +399,7 @@
                 pltpu.VMEM((4, line, cols2, lanes), F32),
                 pltpu.VMEM((half_rows, chan, lanes), BF16),
                 pltpu.VMEM((half_rows, chan, cols2), F32),
-                pltpu.VMEM((half_rows, chan, lanes), F32),
+                pltpu.VMEM((half_rows, chan, 2 * cols2), F32),
                 pltpu.VMEM((half_rows, 1, lanes), F32),
                 pltpu.VMEM((half_rows, 1, lanes), F32),
                 pltpu.VMEM((half_rows, cols2, chan), BF16),
@@ -387,8 +410,8 @@
                 dma((2, 2, line)),
                 dma((chips,)),
                 dma((chips,)),
-                dma((4,)),
-                dma((4,)),
+                dma((7,)),
+                dma((7,)),
             ],
             compiler_params=pltpu.CompilerParams(
                 collective_id=0, has_side_effects=True

time: 43.3 us -> 39.1 us (0.903)
  Pallas kernels: 41 us -> 36.8 us
    pallas_call x1, Pallas kernels: 41 us -> 36.8 us  [on_device(): pl.pallas_call(functools.partial(body, line), out_shape=jax.ShapeDtypeStr...]
where the time goes in v4:
time: 39.1 us; the launch traced here: 39 us
  Pallas kernels  36.8 us (94%)
  local copies, waits for them, and re-layouts  1.57 us (4%)
  between operations  0.66 us (2%)
    pallas_call x1, Pallas kernels, on_device(): pl.pallas_call(functools.partial(body, line), out_shape=jax.ShapeDtypeStr...  36.8 us
    unnamed x1, local copies, waits for them, and re-layouts  1.57 us

profile of v4, /device:TPU:0, one launch (start us, length us, event | category | flops | bytes accessed | tf_op | source)
XLA Modules:
  0.0 39.0 jit_solution(241690816792088104)
XLA Ops:
  0.7 36.8 %shard_map.73 = bf16[16,32,128]{2,1,0:T(8,128)(2,1)} custom-call(bf16[16,32,128]{2,1,0:T(8,128)(2,1)} %pair_in.1, bf16[128,128]{1,0:T(8,128)(2,1)} %wq_in.1, bf16[128,256]{1,0:T(8,128)(2,1)} %wkv_in.1, bf16[128,128]{1,0:T(8,128)(2,1)} %wg_in.1, bf16[128,128]{1,0:T(8,128)(2,1)} %wo_in.1, bf16[4,32,1024]{2,1,0:T(8,128)(2,1)} %bias_in.1, s32[1]{0:T(128)S(6)} %copy.9.len_ref), custom_call_target="tpu_custom_call" | custom-call | flops 3000000000 | bytes 1000000 | tf_op jit(solution)/shard_map/pallas_call | solution.py:382
  37.4 1.6 %copy.10 = bf16[16,32,128]{2,1,0:T(8,128)(2,1)} copy(bf16[16,32,128]{2,1,0:T(8,128)(2,1)} %shard_map.73) | data formatting | bytes 262144

commit v5 on v0

v5 whole, which is shorter than its diff:
```python
import functools

import jax
import jax.numpy as jnp
from jax import lax
from jax.experimental import pallas as pl
from jax.experimental.pallas import tpu as pltpu
from jax.sharding import PartitionSpec as P

HEADS = 4
PEERS = 4
SIDES = 2
MESH = pl.DeviceIdType.MESH
F32 = jnp.float32
BF16 = jnp.bfloat16
LOG2E = 1.4426950408889634
NT = (((1,), (1,)), ((), ()))


def dot(lhs, rhs):
    return jnp.dot(lhs, rhs, preferred_element_type=F32)


def dot_nt(lhs, rhs):
    return lax.dot_general(lhs, rhs, NT, preferred_element_type=F32)


def transposed(weight):
    return weight.astype(F32).T.astype(BF16)


def body(
    line, pair_in, wq_in, wkv_in, wg_in, wo_in, bias_in, len_ref, out_ref,
    pair_ref, bias_ref, wq_ref, wkv_ref, wg_ref, wo_ref, load_sem,
    gath, swap, bsend, bgath, queries, gate, acc, run_max, run_sum, upd, wvt_ref,
    swap_s, swap_r, z_s, y_s, recv, bias_s, bias_r, share_s, share_r, out_s, out_r,
):
    rows, cols, chan = pair_ref.shape
    part_rows, cols4 = rows // PEERS, PEERS * cols
    half_rows = part_rows // 2
    width = chan // HEADS
    lanes = HEADS * cols4
    quads = SIDES * line

    me = lax.axis_index("col")
    place = lax.rem(me, PEERS)
    quad = me // PEERS
    z = quad // SIDES
    side = lax.rem(quad, SIDES)
    other_side = 1 - side

    def device(z_at, side_at):
        return {"col": (z_at * SIDES + side_at) * PEERS + place}

    def peer(k):
        return lax.rem(place + k, PEERS)

    def peer_device(k):
        return {"col": quad * PEERS + peer(k)}

    loads = [
        pltpu.make_async_copy(source, target, load_sem.at[at])
        for at, (source, target) in enumerate((
            (pair_in, pair_ref), (bias_in, bias_ref), (wq_in, wq_ref),
            (wkv_in, wkv_ref), (wg_in, wg_ref), (wo_in, wo_ref),
        ))
    ]
    for load in loads:
        load.start()

    barrier = pltpu.get_barrier_semaphore()

    def greet(k, carry):
        other = lax.rem(quad + k, quads)
        pl.semaphore_signal(barrier, inc=1, device_id={"col": other * PEERS + place}, device_id_type=MESH)
        return carry

    lax.fori_loop(1, quads, greet, 0)
    for k in range(1, PEERS):
        pl.semaphore_signal(barrier, inc=1, device_id=peer_device(k), device_id_type=MESH)

    loads[0].wait()
    values = pair_ref[...].astype(F32)
    centred = values - jnp.mean(values, axis=-1, keepdims=True)
    variance = jnp.mean(centred * centred, axis=-1, keepdims=True)
    swap[...] = (centred * lax.rsqrt(variance + 1e-05)).astype(BF16)

    pl.semaphore_wait(barrier, quads - 1 + PEERS - 1)

    def cols_of(place_at):
        return pl.ds(pl.multiple_of(place_at * cols, cols), cols)

    def swap_copy(k, from_place):
        return pltpu.make_async_remote_copy(
            src_ref=swap.at[pl.ds(peer(k) * part_rows, part_rows)],
            dst_ref=gath.at[side, z, :, cols_of(from_place), :],
            send_sem=swap_s.at[k], recv_sem=swap_r.at[from_place],
            device_id=peer_device(k), device_id_type=MESH,
        )

    for k in range(1, PEERS):
        swap_copy(k, place).start()
    gath[side, z, :, cols_of(place), :] = swap[pl.ds(place * part_rows, part_rows)]

    loads[1].wait()
    for at in range(quads):
        for h in range(HEADS):
            bsend[at, :, h * cols4 : (h + 1) * cols4] = bias_ref[h, :, at * cols4 : (at + 1) * cols4]
    bgath[side, z, cols_of(place), :] = bsend[quad]

    def share_copy(side_at, z_at, k, from_place):
        block = bgath.at[side_at, z_at, cols_of(from_place), :]
        return pltpu.make_async_remote_copy(
            src_ref=block, dst_ref=block,
            send_sem=share_s.at[side_at, z_at, k], recv_sem=share_r.at[side_at, z_at, from_place],
            device_id=peer_device(k), device_id_type=MESH,
        )

    def share(side_at, z_at):
        for k in range(1, PEERS):
            share_copy(side_at, z_at, k, place).start()

    for k in range(1, PEERS):
        swap_copy(k, peer(k)).wait_recv()

    def block_copy(half, side_at, z_at, target, send_sem):
        block = gath.at[side_at, z_at, pl.ds(half * half_rows, half_rows)]
        return pltpu.make_async_remote_copy(
            src_ref=block, dst_ref=block, send_sem=send_sem, recv_sem=recv.at[half, side_at, z_at],
            device_id=target, device_id_type=MESH,
        )

    def up(half, z_at):
        return block_copy(half, side, z_at, device(z + 1, side), z_s.at[half, 0, z_at])

    def down(half, z_at):
        return block_copy(half, side, z_at, device(z - 1, side), z_s.at[half, 1, z_at])

    def across(half, z_at):
        return block_copy(half, side, z_at, device(z, other_side), y_s.at[half, z_at])

    def arrived(half, side_at, z_at):
        block_copy(half, side_at, z_at, device(z, other_side), y_s.at[half, z_at]).wait_recv()

    def forward(half, z_at):
        pl.when((z + 1 < line) & (z_at <= z))(lambda: up(half, z_at).start())
        pl.when((z > 0) & (z_at >= z))(lambda: down(half, z_at).start())
        across(half, z_at).start()

    for half in range(2):
        forward(half, z)

    margin = jnp.minimum(z, line - 1 - z)

    def ranked(at):
        step = (at + 1) // 2
        close = jnp.where(lax.rem(at, 2) == 1, z + step, z - step)
        rest = jnp.where(z == margin, at, line - 1 - at)
        return jnp.where(at <= 2 * margin, close, rest)

    def bias_copy(side_to, z_to, side_from, z_from):
        return pltpu.make_async_remote_copy(
            src_ref=bsend.at[z_to * SIDES + side_to], dst_ref=bgath.at[side_from, z_from, cols_of(place), :],
            send_sem=bias_s.at[side_to, z_to], recv_sem=bias_r.at[side_from, z_from],
            device_id=device(z_to, side_to), device_id_type=MESH,
        )

    def send_bias(side_to, first):
        def one(at, carry):
            bias_copy(side_to, ranked(at), side, z).start()
            return carry

        lax.fori_loop(first, line, one, 0)

    share(side, z)
    send_bias(side, 1)
    send_bias(other_side, 0)

    for load in loads[2:]:
        load.wait()
    wqt = transposed(wq_ref[...])
    wgt = transposed(wg_ref[...])
    wvt_ref[...] = transposed(wkv_ref[:, chan:])
    head_of = lax.broadcasted_iota(jnp.int32, (chan, cols4), 0) // width
    own = gath[side, z].reshape(part_rows * cols4, chan)
    all_queries = (dot_nt(wqt, own) * width ** (-0.5)).astype(BF16).astype(F32)
    all_gates = jax.nn.sigmoid(dot_nt(wgt, own))
    for r in range(part_rows):
        span = slice(r * cols4, (r + 1) * cols4)
        gate[r] = all_gates[:, span]
        for h in range(HEADS):
            one_head = jnp.where(head_of == h, all_queries[:, span], 0.0)
            queries[r, :, h * cols4 : (h + 1) * cols4] = one_head.astype(BF16)

    run_max[...] = jnp.full_like(run_max, -1e30)
    run_sum[...] = jnp.zeros_like(run_sum)
    acc[...] = jnp.zeros_like(acc)
    limit = len_ref[0]

    def fold(side_at, z_at):
        for k in range(1, PEERS):
            share_copy(side_at, z_at, k, peer(k)).wait_recv()
        tiles = gath[side_at, z_at].reshape(part_rows * cols4, chan)
        olds = [(run_max[r], run_sum[r], acc[r]) for r in range(part_rows)]
        position = (z_at * SIDES + side_at) * cols4 + lax.broadcasted_iota(jnp.int32, (cols4, lanes), 0)
        mask = jnp.where(position < limit, 0.0, -1000000000.0)
        bias_tile = (bgath[side_at, z_at].astype(F32) + mask) * LOG2E
        all_keys = dot(tiles, wkv_ref[:, :chan]).astype(BF16)
        all_values = dot_nt(wvt_ref[...], tiles).astype(BF16)
        news = []
        for r, (old_max, old_sum, old_acc) in enumerate(olds):
            span = slice(r * cols4, (r + 1) * cols4)
            scores = dot(all_keys[span], queries[r]) * LOG2E + bias_tile
            new_max = jnp.maximum(old_max, jnp.max(scores, axis=0, keepdims=True))
            rescale = jnp.exp2(old_max - new_max)
            expon = jnp.exp2(scores - new_max)
            total = old_sum * rescale + jnp.sum(expon, axis=0, keepdims=True)
            weights = expon.astype(BF16)
            result = []
            for h in range(0, HEADS, 2):
                both = dot(
                    all_values[h * width : (h + 2) * width, span],
                    weights[:, h * cols4 : (h + 2) * cols4],
                )
                for which in range(2):
                    at = slice((h + which) * width, (h + which + 1) * width)
                    scale = rescale[:, (h + which) * cols4 : (h + which + 1) * cols4]
                    part = both[which * width : (which + 1) * width, which * cols4 : (which + 1) * cols4]
                    result.append(old_acc[at] * scale + part)
            news.append((new_max, total, jnp.concatenate(result, axis=0)))
        for r, new in enumerate(news):
            run_max[r], run_sum[r], acc[r] = new

    def take_bias(side_at, z_at):
        bias_copy(side_at, z_at, side_at, z_at).wait_recv()
        share(side_at, z_at)

    def advance(at, carry):
        z_at = ranked(at)
        for half in range(2):
            arrived(half, side, z_at)
            forward(half, z_at)
        take_bias(side, z_at)
        take_bias(other_side, ranked(at - 1))
        fold(side, ranked(at - 1))
        return carry

    lax.fori_loop(1, line, advance, 0)
    take_bias(other_side, ranked(line - 1))

    def late(at, carry):
        side_at = jnp.where(at == 0, side, other_side)
        z_at = ranked(jnp.where(at == 0, line - 1, at - 1))

        def wait_blocks():
            for half in range(2):
                arrived(half, other_side, z_at)

        pl.when(at > 0)(wait_blocks)
        fold(side_at, z_at)
        return carry

    lax.fori_loop(0, line + 1, late, 0)

    hiddens = []
    for r in range(part_rows):
        scale = 1.0 / run_sum[r]
        attended = jnp.concatenate(
            [
                acc[r, h * width : (h + 1) * width] * scale[:, h * cols4 : (h + 1) * cols4]
                for h in range(HEADS)
            ],
            axis=0,
        )
        hiddens.append((gate[r] * attended).T.astype(BF16))
    update = dot(jnp.concatenate(hiddens, axis=0), wo_ref[...]).astype(BF16)
    upd[...] = update.reshape(part_rows, cols4, chan)

    def out_copy(k, from_place):
        return pltpu.make_async_remote_copy(
            src_ref=upd.at[:, cols_of(peer(k)), :],
            dst_ref=out_ref.at[pl.ds(from_place * part_rows, part_rows)],
            send_sem=out_s.at[k], recv_sem=out_r.at[from_place],
            device_id=peer_device(k), device_id_type=MESH,
        )

    for k in range(1, PEERS):
        out_copy(k, place).start()
    out_ref[pl.ds(place * part_rows, part_rows)] = upd[:, cols_of(place), :]

    for k in range(1, PEERS):
        swap_copy(k, place).wait_send()
    for half in range(2):
        for z_at in range(line):
            pl.when((z + 1 < line) & (z_at <= z))(lambda: up(half, z_at).wait_send())
            pl.when((z > 0) & (z_at >= z))(lambda: down(half, z_at).wait_send())
            across(half, z_at).wait_send()

    def drain(at, carry):
        side_at, z_at = at // line, lax.rem(at, line)
        pl.when((side_at != side) | (z_at != z))(lambda: bias_copy(side_at, z_at, side, z).wait_send())
        for k in range(1, PEERS):
            share_copy(side_at, z_at, k, place).wait_send()
        return carry

    lax.fori_loop(0, quads, drain, 0)
    for k in range(1, PEERS):
        out_copy(k, place).wait_send()
        out_copy(k, peer(k)).wait_recv()


def solution(mesh):
    quads = mesh.shape["col"] // PEERS
    line = quads // SIDES

    def on_device(pair, w_query, w_kv, w_gate, w_out, pair_bias, lengths):
        rows, cols, chan = pair.shape
        part_rows, cols4 = rows // PEERS, PEERS * cols
        lanes = HEADS * cols4
        vmem = pl.BlockSpec(memory_space=pltpu.VMEM)
        dma = pltpu.SemaphoreType.DMA
        return pl.pallas_call(
            functools.partial(body, line),
            out_shape=jax.ShapeDtypeStruct(pair.shape, BF16),
            in_specs=[pl.BlockSpec(memory_space=pl.ANY)] * 6 + [pl.BlockSpec(memory_space=pltpu.SMEM)],
            out_specs=vmem,
            scratch_shapes=[
                pltpu.VMEM(pair.shape, BF16),
                pltpu.VMEM(pair_bias.shape, BF16),
                pltpu.VMEM(w_query.shape, BF16),
                pltpu.VMEM(w_kv.shape, BF16),
                pltpu.VMEM(w_gate.shape, BF16),
                pltpu.VMEM(w_out.shape, BF16),
                dma((6,)),
                pltpu.VMEM((SIDES, line, part_rows, cols4, chan), BF16),
                pltpu.VMEM((rows, cols, chan), BF16),
                pltpu.VMEM((quads, cols, lanes), BF16),
                pltpu.VMEM((SIDES, line, cols4, lanes), BF16),
                pltpu.VMEM((part_rows, chan, lanes), BF16),
                pltpu.VMEM((part_rows, chan, cols4), F32),
                pltpu.VMEM((part_rows, chan, cols4), F32),
                pltpu.VMEM((part_rows, 1, lanes), F32),
                pltpu.VMEM((part_rows, 1, lanes), F32),
                pltpu.VMEM((part_rows, cols4, chan), BF16),
                pltpu.VMEM((chan, chan), BF16),
                dma((PEERS,)),
                dma((PEERS,)),
                dma((2, 2, line)),
                dma((2, line)),
                dma((2, SIDES, line)),
                dma((SIDES, line)),
                dma((SIDES, line)),
                dma((SIDES, line, PEERS)),
                dma((SIDES, line, PEERS)),
                dma((PEERS,)),
                dma((PEERS,)),
            ],
            compiler_params=pltpu.CompilerParams(collective_id=0, has_side_effects=True),
            cost_estimate=pl.CostEstimate(flops=3 * 10**9, bytes_accessed=10**6, transcendentals=2 * 10**6),
        )(pair, w_query, w_kv, w_gate, w_out, pair_bias, lengths)

    in_specs = (P("grp", "col", None), P(), P(), P(), P(), P("grp", "col", None), P("grp"))
    return jax.shard_map(
        on_device, mesh=mesh, in_specs=in_specs, out_specs=P("grp", "col", None), check_vma=False
    )
```

time: 115 us -> 42.8 us (0.37)
  waiting for transfers between devices: 52.3 us -> 0 us
  Pallas kernels: 0 us -> 40.4 us
  matrix products: 21.1 us -> 0 us
  between operations: 13.5 us -> 0.66 us
  local copies, waits for them, and re-layouts: 11.1 us -> 1.57 us
  other arithmetic: 8.07 us -> 0 us
  starting transfers between devices: 7.3 us -> 0 us
  loops' own time: 1.31 us -> 0 us
    all_gather x1 -> x0, waiting for transfers between devices: 43.4 us -> none  [gather_keys(): lax.all_gather(normed, 'col', axis=1, tiled=True)]
    pallas_call x0 -> x1, Pallas kernels: none -> 40.4 us  [on_device(): pl.pallas_call(functools.partial(body, line), out_shape=jax.ShapeDtypeStr...]
    dot_general x8 -> x0, matrix products: 21.1 us -> none  [the longest x2 6.84 us: consume(): jnp.einsum('rhjk,rkhd->rjhd', weights, value_tile, preferred_element_type...]
    all_to_all x1 -> x0, waiting for transfers between devices: 8.85 us -> none  [on_device(): lax.all_to_all(pair_bias, 'col', split_axis=2, concat_axis=1, tiled=True)]
    all_to_all x1 -> x0, starting transfers between devices: 7.3 us -> none  [on_device(): lax.all_to_all(pair_bias, 'col', split_axis=2, concat_axis=1, tiled=True)]
    reduce_sum x4 -> x0, other arithmetic: 4.61 us -> none  [the longest x2 2.38 us: consume(): new_sum = run_sum * rescale + jnp.sum(expon, axis=-1)]
    unnamed x9 -> x1, local copies, waits for them, and re-layouts: 5.46 us -> 1.57 us
    convert_element_type x3 -> x0, other arithmetic: 1.81 us -> none  [the longest x1 1.76 us: normalize(): return (centred * lax.rsqrt(variance + 1e-05)).astype(jnp.bfloat16)]
  transfers between devices with their start and end apart: 2 -> 0, of which waited for: 2 -> 0; matrix products, arithmetic and copies ran while one was open for 7% -> 0% of each run, Pallas kernels for 0% -> 0%
where the time goes in v5:
time: 42.8 us; the launch traced here: 42.6 us
  Pallas kernels  40.4 us (94%)
  local copies, waits for them, and re-layouts  1.57 us (4%)
  between operations  0.66 us (2%)
    pallas_call x1, Pallas kernels, on_device(): pl.pallas_call(functools.partial(body, line), out_shape=jax.ShapeDtypeStr...  40.4 us
    unnamed x1, local copies, waits for them, and re-layouts  1.57 us

profile of v5, /device:TPU:0, one launch (start us, length us, event | category | flops | bytes accessed | tf_op | source)
XLA Modules:
  0.0 42.6 jit_solution(10643366924510037141)
XLA Ops:
  0.7 40.4 %shard_map.73 = bf16[16,32,128]{2,1,0:T(8,128)(2,1)} custom-call(bf16[16,32,128]{2,1,0:T(8,128)(2,1)} %pair_in.1, bf16[128,128]{1,0:T(8,128)(2,1)} %wq_in.1, bf16[128,256]{1,0:T(8,128)(2,1)} %wkv_in.1, bf16[128,128]{1,0:T(8,128)(2,1)} %wg_in.1, bf16[128,128]{1,0:T(8,128)(2,1)} %wo_in.1, bf16[4,32,1024]{2,1,0:T(8,128)(2,1)} %bias_in.1, s32[1]{0:T(128)S(6)} %copy.9.len_ref), custom_call_target="tpu_custom_call" | custom-call | flops 3000000000 | bytes 1000000 | tf_op jit(solution)/shard_map/pallas_call | solution.py:322
  41.1 1.6 %copy.10 = bf16[16,32,128]{2,1,0:T(8,128)(2,1)} copy(bf16[16,32,128]{2,1,0:T(8,128)(2,1)} %shard_map.73) | data formatting | bytes 262144

commit v6 on v5

--- a/solution.py
+++ b/solution.py
@@ -243,6 +243,13 @@
         take_bias(side, z_at)
         take_bias(other_side, ranked(at - 1))
         fold(side, ranked(at - 1))
+
+        def cross():
+            for half in range(2):
+                arrived(half, other_side, ranked(at - 2))
+            fold(other_side, ranked(at - 2))
+
+        pl.when(at > 1)(cross)
         return carry
 
     lax.fori_loop(1, line, advance, 0)
@@ -250,7 +257,7 @@
 
     def late(at, carry):
         side_at = jnp.where(at == 0, side, other_side)
-        z_at = ranked(jnp.where(at == 0, line - 1, at - 1))
+        z_at = ranked(jnp.where(at == 0, line - 1, line - 3 + at))
 
         def wait_blocks():
             for half in range(2):
@@ -260,7 +267,7 @@
         fold(side_at, z_at)
         return carry
 
-    lax.fori_loop(0, line + 1, late, 0)
+    lax.fori_loop(0, 3, late, 0)
 
     hiddens = []
     for r in range(part_rows):

time: 42.8 us -> 41 us (0.958)
  Pallas kernels: 40.4 us -> 38.6 us
    pallas_call x1, Pallas kernels: 40.4 us -> 38.6 us  [on_device(): pl.pallas_call(functools.partial(body, line), out_shape=jax.ShapeDtypeStr...]
where the time goes in v6:
time: 41 us; the launch traced here: 40.8 us
  Pallas kernels  38.6 us (94%)
  local copies, waits for them, and re-layouts  1.57 us (4%)
  between operations  0.66 us (2%)
    pallas_call x1, Pallas kernels, on_device(): pl.pallas_call(functools.partial(body, line), out_shape=jax.ShapeDtypeStr...  38.6 us
    unnamed x1, local copies, waits for them, and re-layouts  1.57 us

profile of v6, /device:TPU:0, one launch (start us, length us, event | category | flops | bytes accessed | tf_op | source)
XLA Modules:
  0.0 40.8 jit_solution(14831699329281761085)
XLA Ops:
  0.7 38.6 %shard_map.73 = bf16[16,32,128]{2,1,0:T(8,128)(2,1)} custom-call(bf16[16,32,128]{2,1,0:T(8,128)(2,1)} %pair_in.1, bf16[128,128]{1,0:T(8,128)(2,1)} %wq_in.1, bf16[128,256]{1,0:T(8,128)(2,1)} %wkv_in.1, bf16[128,128]{1,0:T(8,128)(2,1)} %wg_in.1, bf16[128,128]{1,0:T(8,128)(2,1)} %wo_in.1, bf16[4,32,1024]{2,1,0:T(8,128)(2,1)} %bias_in.1, s32[1]{0:T(128)S(6)} %copy.9.len_ref), custom_call_target="tpu_custom_call" | custom-call | flops 3000000000 | bytes 1000000 | tf_op jit(solution)/shard_map/pallas_call | solution.py:329
  39.3 1.6 %copy.10 = bf16[16,32,128]{2,1,0:T(8,128)(2,1)} copy(bf16[16,32,128]{2,1,0:T(8,128)(2,1)} %shard_map.73) | data formatting | bytes 262144

commit v7 on v5

--- a/solution.py
+++ b/solution.py
@@ -150,13 +150,18 @@
     for half in range(2):
         forward(half, z)
 
-    margin = jnp.minimum(z, line - 1 - z)
+    group = line // 2
+    near_part = z // group
+    inside = z - near_part * group
+    margin = jnp.minimum(inside, group - 1 - inside)
 
     def ranked(at):
         step = (at + 1) // 2
-        close = jnp.where(lax.rem(at, 2) == 1, z + step, z - step)
-        rest = jnp.where(z == margin, at, line - 1 - at)
-        return jnp.where(at <= 2 * margin, close, rest)
+        close = jnp.where(lax.rem(at, 2) == 1, inside + step, inside - step)
+        rest = jnp.where(inside == margin, at, group - 1 - at)
+        near = near_part * group + jnp.where(at <= 2 * margin, close, rest)
+        far = jnp.where(near_part == 0, at, line - 1 - at)
+        return jnp.where(at < group, near, far)
 
     def bias_copy(side_to, z_to, side_from, z_from):
         return pltpu.make_async_remote_copy(
@@ -197,19 +202,26 @@
     acc[...] = jnp.zeros_like(acc)
     limit = len_ref[0]
 
-    def fold(side_at, z_at):
-        for k in range(1, PEERS):
-            share_copy(side_at, z_at, k, peer(k)).wait_recv()
-        tiles = gath[side_at, z_at].reshape(part_rows * cols4, chan)
+    keys = 2 * cols4
+
+    def fold(side_at, first):
+        z_at = pl.ds(first, 2)
+        for block in range(2):
+            for k in range(1, PEERS):
+                share_copy(side_at, first + block, k, peer(k)).wait_recv()
+        tiles = jnp.concatenate(
+            [gath[side_at, z_at, r].reshape(keys, chan) for r in range(part_rows)], axis=0
+        )
+        position = lax.broadcasted_iota(jnp.int32, (2, cols4, lanes), 1)
+        position = position + lax.broadcasted_iota(jnp.int32, (2, cols4, lanes), 0) * SIDES * cols4
+        mask = jnp.where(position < limit - (first * SIDES + side_at) * cols4, 0.0, -1000000000.0)
+        bias_tile = ((bgath[side_at, z_at].astype(F32) + mask) * LOG2E).reshape(keys, lanes)
         olds = [(run_max[r], run_sum[r], acc[r]) for r in range(part_rows)]
-        position = (z_at * SIDES + side_at) * cols4 + lax.broadcasted_iota(jnp.int32, (cols4, lanes), 0)
-        mask = jnp.where(position < limit, 0.0, -1000000000.0)
-        bias_tile = (bgath[side_at, z_at].astype(F32) + mask) * LOG2E
         all_keys = dot(tiles, wkv_ref[:, :chan]).astype(BF16)
         all_values = dot_nt(wvt_ref[...], tiles).astype(BF16)
         news = []
         for r, (old_max, old_sum, old_acc) in enumerate(olds):
-            span = slice(r * cols4, (r + 1) * cols4)
+            span = slice(r * keys, (r + 1) * keys)
             scores = dot(all_keys[span], queries[r]) * LOG2E + bias_tile
             new_max = jnp.maximum(old_max, jnp.max(scores, axis=0, keepdims=True))
             rescale = jnp.exp2(old_max - new_max)
@@ -235,6 +247,22 @@
         bias_copy(side_at, z_at, side_at, z_at).wait_recv()
         share(side_at, z_at)
 
+    def fold_half(side_at, part):
+        def one(at, carry):
+            fold(side_at, part * group + 2 * at)
+            return carry
+
+        lax.fori_loop(0, group // 2, one, 0)
+
+    def fold_other(part):
+        def one(at, carry):
+            for half in range(2):
+                arrived(half, other_side, part * group + at)
+            return carry
+
+        lax.fori_loop(0, group, one, 0)
+        fold_half(other_side, part)
+
     def advance(at, carry):
         z_at = ranked(at)
         for half in range(2):
@@ -242,25 +270,14 @@
             forward(half, z_at)
         take_bias(side, z_at)
         take_bias(other_side, ranked(at - 1))
-        fold(side, ranked(at - 1))
+        pl.when(at == group - 1)(lambda: fold_half(side, near_part))
+        pl.when(at == line - 2)(lambda: fold_other(near_part))
         return carry
 
     lax.fori_loop(1, line, advance, 0)
     take_bias(other_side, ranked(line - 1))
-
-    def late(at, carry):
-        side_at = jnp.where(at == 0, side, other_side)
-        z_at = ranked(jnp.where(at == 0, line - 1, at - 1))
-
-        def wait_blocks():
-            for half in range(2):
-                arrived(half, other_side, z_at)
-
-        pl.when(at > 0)(wait_blocks)
-        fold(side_at, z_at)
-        return carry
-
-    lax.fori_loop(0, line + 1, late, 0)
+    fold_half(side, 1 - near_part)
+    fold_other(1 - near_part)
 
     hiddens = []
     for r in range(part_rows):

time: 42.8 us -> 46.2 us (1.079)
  Pallas kernels: 40.4 us -> 43.8 us
    pallas_call x1, Pallas kernels: 40.4 us -> 43.8 us  [on_device(): pl.pallas_call(functools.partial(body, line), out_shape=jax.ShapeDtypeStr...]
where the time goes in v7:
time: 46.2 us; the launch traced here: 46.1 us
  Pallas kernels  43.8 us (95%)
  local copies, waits for them, and re-layouts  1.57 us (3%)
  between operations  0.66 us (1%)
    pallas_call x1, Pallas kernels, on_device(): pl.pallas_call(functools.partial(body, line), out_shape=jax.ShapeDtypeStr...  43.8 us
    unnamed x1, local copies, waits for them, and re-layouts  1.57 us

profile of v7, /device:TPU:0, one launch (start us, length us, event | category | flops | bytes accessed | tf_op | source)
XLA Modules:
  0.0 46.1 jit_solution(6294857462910573828)
XLA Ops:
  0.7 43.8 %shard_map.73 = bf16[16,32,128]{2,1,0:T(8,128)(2,1)} custom-call(bf16[16,32,128]{2,1,0:T(8,128)(2,1)} %pair_in.1, bf16[128,128]{1,0:T(8,128)(2,1)} %wq_in.1, bf16[128,256]{1,0:T(8,128)(2,1)} %wkv_in.1, bf16[128,128]{1,0:T(8,128)(2,1)} %wg_in.1, bf16[128,128]{1,0:T(8,128)(2,1)} %wo_in.1, bf16[4,32,1024]{2,1,0:T(8,128)(2,1)} %bias_in.1, s32[1]{0:T(128)S(6)} %copy.9.len_ref), custom_call_target="tpu_custom_call" | custom-call | flops 3000000000 | bytes 1000000 | tf_op jit(solution)/shard_map/pallas_call | solution.py:339
  44.5 1.6 %copy.10 = bf16[16,32,128]{2,1,0:T(8,128)(2,1)} copy(bf16[16,32,128]{2,1,0:T(8,128)(2,1)} %shard_map.73) | data formatting | bytes 262144

commit v8 on v4

--- a/solution.py
+++ b/solution.py
@@ -288,6 +288,16 @@
 
         lax.fori_loop(0, 2, one, 0)
 
+    def late(unit, carry):
+        half, stage = lax.rem(unit, 2), unit // 2
+        line_at = jnp.where(stage < 2, pick(half, far), diag)
+        part = jnp.where(lax.rem(stage, 2) == 0, own_part, 1 - own_part)
+        for z_at in range(group):
+            block = gath.at[line_at, part * group + z_at, pl.ds(half * quarter, quarter)]
+            pltpu.make_async_copy(block, block, recv.at[half, line_at, part * group + z_at]).wait()
+        fold(half, line_at, part)
+        return carry
+
     own = (xy, xy)
     for s in range(1, line):
         pass_line(s)
@@ -303,6 +313,7 @@
             spread_bias(1)
             spread_bias(2)
             fold_both(near, own_part)
+            lax.fori_loop(0, 2, late, 0)
         else:
             pass_near(s - 1)
     start_bias(3)
@@ -311,17 +322,7 @@
     spread_bias(3)
     fold_both(near, 1 - own_part)
 
-    def late(unit, carry):
-        half, stage = lax.rem(unit, 2), unit // 2
-        line_at = jnp.where(stage < 2, pick(half, far), diag)
-        part = jnp.where(lax.rem(stage, 2) == 0, own_part, 1 - own_part)
-        for z_at in range(group):
-            block = gath.at[line_at, part * group + z_at, pl.ds(half * quarter, quarter)]
-            pltpu.make_async_copy(block, block, recv.at[half, line_at, part * group + z_at]).wait()
-        fold(half, line_at, part)
-        return carry
-
-    lax.fori_loop(0, 7, late, 0)
+    lax.fori_loop(2, 7, late, 0)
 
     other_cols = pl.ds(pl.multiple_of((1 - core) * cols, cols), cols)
 

time: 39.1 us -> 38.1 us (0.974)
  Pallas kernels: 36.8 us -> 35.7 us
    pallas_call x1, Pallas kernels: 36.8 us -> 35.7 us  [on_device(): pl.pallas_call(functools.partial(body, line), out_shape=jax.ShapeDtypeStr...]
where the time goes in v8:
time: 38.1 us; the launch traced here: 37.9 us
  Pallas kernels  35.7 us (94%)
  local copies, waits for them, and re-layouts  1.57 us (4%)
  between operations  0.66 us (2%)
    pallas_call x1, Pallas kernels, on_device(): pl.pallas_call(functools.partial(body, line), out_shape=jax.ShapeDtypeStr...  35.7 us
    unnamed x1, local copies, waits for them, and re-layouts  1.57 us

profile of v8, /device:TPU:0, one launch (start us, length us, event | category | flops | bytes accessed | tf_op | source)
XLA Modules:
  0.0 37.9 jit_solution(16975953107945824846)
XLA Ops:
  0.7 35.7 %shard_map.73 = bf16[16,32,128]{2,1,0:T(8,128)(2,1)} custom-call(bf16[16,32,128]{2,1,0:T(8,128)(2,1)} %pair_in.1, bf16[128,128]{1,0:T(8,128)(2,1)} %wq_in.1, bf16[128,256]{1,0:T(8,128)(2,1)} %wkv_in.1, bf16[128,128]{1,0:T(8,128)(2,1)} %wg_in.1, bf16[128,128]{1,0:T(8,128)(2,1)} %wo_in.1, bf16[4,32,1024]{2,1,0:T(8,128)(2,1)} %bias_in.1, s32[1]{0:T(128)S(6)} %copy.9.len_ref), custom_call_target="tpu_custom_call" | custom-call | flops 3000000000 | bytes 1000000 | tf_op jit(solution)/shard_map/pallas_call | solution.py:383
  36.4 1.6 %copy.10 = bf16[16,32,128]{2,1,0:T(8,128)(2,1)} copy(bf16[16,32,128]{2,1,0:T(8,128)(2,1)} %shard_map.73) | data formatting | bytes 262144
